TPU v7x, 256 devices: a whole 4x4x8 slice. The times are simulated.
256 devices in a mesh: row: 32 (over z, y_lo, core), col: 8 (over y_hi, x).
Axes of the slice: x: 4, y: 4 (y_hi: 2, y_lo: 2; y = y_hi * 2 + y_lo), z: 8, core: 2. Of those that a mesh axis runs over, the one named last changes fastest.
Arguments:
- single: bfloat16 [10, 2048, 768], P(None, ('row', 'col')), may hold values from -6 to 6
- pair_bias: bfloat16 [2048, 64, 512], P('row', 'col'), may hold values from -250 to 250
- token_gain: float32 [768], replicated, may hold values from 0.1 to 1.9
- w_query: bfloat16 [768, 768], replicated, may hold values from -0.21875 to 0.21875
- w_key: bfloat16 [768, 768], replicated, may hold values from -0.21875 to 0.21875
- w_value: bfloat16 [768, 768], replicated, may hold values from -0.21875 to 0.21875
- w_gate: bfloat16 [768, 768], replicated, may hold values from -0.21875 to 0.21875
- w_out: bfloat16 [768, 768], replicated, may hold values from -0.875 to 0.875
- w_cond: bfloat16 [768, 128], replicated, may hold values from -0.21875 to 0.21875
- atom_single: bfloat16 [10, 32768, 128], P(None, ('row', 'col')), may hold values from -6 to 6
- atom_token: int32 [32768], P(('row', 'col')), may hold values from 0 to 2047, as said below
- atom_bias: bfloat16 [1024, 32, 512], P(('row', 'col')), may hold values from -250 to 250
- atom_gain: float32 [128], replicated, may hold values from 0.1 to 1.9
- atom_query: bfloat16 [128, 128], replicated, may hold values from -0.5 to 0.5
- atom_key: bfloat16 [128, 128], replicated, may hold values from -0.5 to 0.5
- atom_value: bfloat16 [128, 128], replicated, may hold values from -0.5 to 0.5
- atom_gate: bfloat16 [128, 128], replicated, may hold values from -0.5 to 0.5
- atom_out: bfloat16 [128, 128], replicated, may hold values from -1 to 1
- pool_gain: float32 [128], replicated, may hold values from 0.1 to 1.9
- w_pool: bfloat16 [128, 768], replicated, may hold values from -0.5 to 0.5
Outputs:
- token_update: bfloat16 [10, 2048, 768], P(None, ('row', 'col'))
- atom_result: bfloat16 [10, 32768, 128], P(None, ('row', 'col'))
- token_pool: bfloat16 [10, 2048, 768], P(None, ('row', 'col'))
Inputs may be any that keep to these rules, and one draw needn't show every extreme that they name: atom_token never falls along the atoms, every token has at least one atom, and the atoms of the block of 128 atoms numbered k belong to tokens of the blocks of 8 tokens numbered k - 1 and k; for k >= 1 the first 16 or more of them belong to block k - 1.
All inputs are finite; a program needn't handle non-finite values.
Results may differ from a plain program's by a relative error of at most 0.029.
Values may be sent and summed in bfloat16 or wider, within the bound.
A program may use at most 128 MiB of HBM per device.

v0:
```python
import math

import jax
import jax.numpy as jnp
from jax import lax
from jax.sharding import PartitionSpec as P

WQ = 32
WK = 128


EPSILON = 1e-05


def shifted(block, axis, distance):
    devices = range(lax.axis_size(axis))
    route = [(i - distance, i) for i in devices if i - distance in devices]
    return lax.ppermute(block, axis, route)


def extended(array, sides, width):
    for axis, dim in sides:
        count, length = (lax.axis_size(axis), array.shape[dim])
        up = [(i, (i + 1) % count) for i in range(count - 1)]
        down = [(j, i) for i, j in up]
        last = lax.slice_in_dim(array, length - width, length, axis=dim)
        initial = lax.slice_in_dim(array, 0, width, axis=dim)
        before = lax.ppermute(last, axis, up)
        after = lax.ppermute(initial, axis, down)
        array = jnp.concatenate([before, array, after], axis=dim)
    return array


def layer_norm(inputs, gain):
    values = inputs.astype(jnp.float32)
    center = values - jnp.mean(values, axis=-1, keepdims=True)
    spread = jnp.mean(center * center, axis=-1, keepdims=True)
    return center * lax.rsqrt(spread + EPSILON) * gain


def matmul(inputs, weight):
    flat = inputs.reshape(-1, inputs.shape[-1])
    result = jnp.dot(flat, weight, preferred_element_type=jnp.float32)
    return result.reshape(inputs.shape[:-1] + (weight.shape[1],))


def on_device(
    single,
    pair_bias,
    token_gain,
    w_query,
    w_key,
    w_value,
    w_gate,
    w_out,
    w_cond,
    atom_single,
    atom_token,
    atom_bias,
    atom_gain,
    atom_query,
    atom_key,
    atom_value,
    atom_gate,
    atom_out,
    pool_gain,
    w_pool,
):
    n_row = lax.axis_size("row")
    n_col = lax.axis_size("col")
    samples, tok_dev, width = single.shape
    heads = pair_bias.shape[2] // n_row
    head_dim = width // heads
    block_rows = tok_dev * n_col
    tile_keys = tok_dev * n_row
    scale = 1.0 / math.sqrt(head_dim)
    normed = layer_norm(single, token_gain).astype(jnp.bfloat16)
    query = matmul(normed, w_query).astype(jnp.bfloat16)
    gate_lin = matmul(normed, w_gate).astype(jnp.bfloat16)
    query_block = lax.all_gather(query, "col", axis=1, tiled=True)
    key_part = matmul(normed, w_key).astype(jnp.bfloat16)
    value_part = matmul(normed, w_value).astype(jnp.bfloat16)
    key_block, value_block = (
        lax.all_gather(key_part, "row", axis=1, tiled=True),
        lax.all_gather(value_part, "row", axis=1, tiled=True),
    )
    bias_tile = jnp.transpose(
        pair_bias.reshape(block_rows, tok_dev, n_row, heads), (3, 0, 2, 1)
    ).reshape(heads, block_rows, tile_keys)
    query_heads = query_block.reshape(samples, block_rows, heads, head_dim)
    key_heads = key_block.reshape(samples, tile_keys, heads, head_dim)
    value_heads = value_block.reshape(samples, tile_keys, heads, head_dim)

    def score_one(members):
        query_one, key_one = members
        raw = jnp.einsum("qhd,khd->hqk", query_one, key_one, preferred_element_type=jnp.float32)
        return raw * scale + bias_tile.astype(jnp.float32)

    scores = lax.map(score_one, (query_heads, key_heads))
    tile_max = jnp.max(scores, axis=-1)

    def weigh_one(members):
        scores_one, maxima_one, value_one = members
        weights = jnp.exp(scores_one - maxima_one[:, :, None])
        totals = jnp.sum(weights, axis=-1)
        mixed = jnp.einsum(
            "hqk,khd->qhd",
            weights.astype(jnp.bfloat16),
            value_one,
            preferred_element_type=jnp.float32,
        )
        return (mixed.reshape(block_rows, width), totals)

    maxima = lax.pmax(tile_max.astype(jnp.bfloat16), "col").astype(tile_max.dtype)
    mixed_all, totals_all = lax.map(weigh_one, (scores, maxima, value_heads))
    mixed_own, totals_own = (
        lax.psum_scatter(
            mixed_all.astype(jnp.bfloat16), "col", scatter_dimension=1, tiled=True
        ).astype(jnp.float32),
        lax.psum_scatter(
            totals_all.astype(jnp.bfloat16), "col", scatter_dimension=2, tiled=True
        ).astype(jnp.float32),
    )
    attended = (
        mixed_own.reshape(samples, tok_dev, heads, head_dim)
        / jnp.transpose(totals_own, (0, 2, 1))[..., None]
    )
    attended = attended.reshape(samples, tok_dev, width)
    gated = (attended * jax.nn.sigmoid(gate_lin.astype(jnp.float32))).astype(jnp.bfloat16)
    token_update = matmul(gated, w_out).astype(jnp.bfloat16)
    cond = matmul(token_update, w_cond).astype(jnp.bfloat16)
    cond_lower = shifted(cond, ("row", "col"), 1)
    cond_rim = jnp.concatenate([cond_lower, cond], axis=1)
    device = lax.axis_index(("row", "col"))
    atom_dev = atom_single.shape[1]
    atom_width = atom_single.shape[2]
    local_token = atom_token - (device - 1) * tok_dev
    selector = (local_token[:, None] == jnp.arange(2 * tok_dev, dtype=jnp.int32)[None, :]).astype(
        jnp.bfloat16
    )
    carried = jnp.einsum("at,stc->sac", selector, cond_rim, preferred_element_type=jnp.float32)
    atom_state = atom_single.astype(jnp.float32) + carried
    atom_normed = layer_norm(atom_state, atom_gain).astype(jnp.bfloat16)
    atom_q = matmul(atom_normed, atom_query).astype(jnp.bfloat16)
    atom_k = matmul(atom_normed, atom_key).astype(jnp.bfloat16)
    atom_v = matmul(atom_normed, atom_value).astype(jnp.bfloat16)
    atom_g = matmul(atom_normed, atom_gate).astype(jnp.bfloat16)
    reach = (WK - WQ) // 2
    kv_rim = extended(jnp.concatenate([atom_k, atom_v], axis=-1), ((("row", "col"), 1),), reach)
    windows = atom_dev // WQ
    kv_window = jnp.stack(
        [
            lax.slice_in_dim(kv_rim, window * WQ, window * WQ + WK, axis=1)
            for window in range(windows)
        ],
        axis=1,
    )
    atom_heads = atom_bias.shape[2] // WK
    atom_hdim = atom_width // atom_heads
    key_window = kv_window[..., :atom_width].reshape(samples, windows, WK, atom_heads, atom_hdim)
    value_window = kv_window[..., atom_width:].reshape(samples, windows, WK, atom_heads, atom_hdim)
    query_window = atom_q.reshape(samples, windows, WQ, atom_heads, atom_hdim)
    total_atoms = atom_dev * n_row * n_col
    position = (
        device * atom_dev
        + jnp.arange(windows, dtype=jnp.int32)[:, None] * WQ
        + jnp.arange(WK, dtype=jnp.int32)[None, :]
        - reach
    )
    valid = (position >= 0) & (position < total_atoms)
    window_bias = jnp.transpose(
        atom_bias.reshape(windows, WQ, atom_heads, WK), (0, 2, 1, 3)
    ).astype(jnp.float32)
    atom_scores = jnp.einsum(
        "swqhd,swkhd->swhqk", query_window, key_window, preferred_element_type=jnp.float32
    )
    atom_scores = atom_scores * (1.0 / math.sqrt(atom_hdim)) + window_bias[None]
    atom_scores = jnp.where(valid[None, :, None, None, :], atom_scores, -1000000000.0)
    atom_maxima = jnp.max(atom_scores, axis=-1, keepdims=True)
    atom_weights = jnp.exp(atom_scores - atom_maxima)
    atom_totals = jnp.sum(atom_weights, axis=-1)
    atom_mixed = jnp.einsum(
        "swhqk,swkhd->swqhd",
        atom_weights.astype(jnp.bfloat16),
        value_window,
        preferred_element_type=jnp.float32,
    )
    atom_mixed = atom_mixed / jnp.transpose(atom_totals, (0, 1, 3, 2))[..., None]
    atom_mixed = atom_mixed.reshape(samples, atom_dev, atom_width)
    atom_gated = (atom_mixed * jax.nn.sigmoid(atom_g.astype(jnp.float32))).astype(jnp.bfloat16)
    atom_result = (atom_state + matmul(atom_gated, atom_out)).astype(jnp.bfloat16)
    sums_local = jnp.einsum(
        "at,sac->stc", selector, atom_result, preferred_element_type=jnp.float32
    )
    from_next = shifted(sums_local[:, :tok_dev].astype(jnp.bfloat16), ("row", "col"), -1).astype(
        jnp.float32
    )
    own_sums = sums_local[:, tok_dev:] + from_next
    pooled = layer_norm(own_sums, pool_gain).astype(jnp.bfloat16)
    token_pool = matmul(pooled, w_pool).astype(jnp.bfloat16)
    return (token_update, atom_result, token_pool)


def solution(mesh):
    placed = (
        P(None, ("row", "col"), None),
        P("row", "col", None),
        P(),
        P(),
        P(),
        P(),
        P(),
        P(),
        P(),
        P(None, ("row", "col"), None),
        P(("row", "col")),
        P(("row", "col"), None, None),
        P(),
        P(),
        P(),
        P(),
        P(),
        P(),
        P(),
        P(),
    )
    return jax.shard_map(
        on_device,
        mesh=mesh,
        in_specs=placed,
        out_specs=(
            P(None, ("row", "col"), None),
            P(None, ("row", "col"), None),
            P(None, ("row", "col"), None),
        ),
        check_vma=False,
    )
```

profile of v0, /device:TPU:6, one launch (start us, length us, event | category | flops | bytes accessed | tf_op | source)
XLA Modules:
  0.0 420.2 jit_solution(13006174932469927282)
XLA Ops:
  11.5 2.4 fusion.43
  14.4 36.3 %all_gather.10 = bf16[10,64,768]{2,1,0:T(8,128)(2,1)S(1)} all-gather(bf16[10,8,768]{2,1,0:T(8,128)(2,1)S(1)} %fusion.46), channel_id=1, replica_groups=mesh['row'=32,'col'=8] {'col'}, dimensions={1}, use_global_device_ids=true | all-gather | bytes 1105920 | tf_op jit(solution)/shard_map/all_gather | solution.py:80
  56.7 24.8 %all-gather.5.cloned.1.call-done = bf16[10,256,768]{2,1,0:T(8,128)(2,1)} async-done(((bf16[10,8,768]{2,1,0:T(8,128)(2,1)}), bf16[10,256,768]{2,1,0:T(8,128)(2,1)}) %all-gather.5.cloned.1.call-update) | async-done | bytes 3932176 | tf_op jit(solution)/shard_map/all_gather | solution.py:84
  81.6 6.3 %copy.92 = bf16[10,256,768]{1,2,0:T(8,128)(2,1)} copy(bf16[10,256,768]{2,1,0:T(8,128)(2,1)} %all-gather.5.cloned.1.call-done) | data formatting | bytes 7864320 | tf_op jit(solution)/shard_map/all_gather | solution.py:84
  87.9 23.5 %while.22 = (s32[]{:T(128)}, f32[10,16,64,256]{3,2,1,0:T(8,128)}, bf16[10,64,16,48]{1,3,2,0:T(8,128)(2,1)S(1)}, bf16[10,256,16,48]{1,3,2,0:T(8,128)(2,1)}, bf16[16,64,256]{2,1,0:T(8,128)(2,1)S(1)}, /*index=5*/s32[]{:T(128)}) while((s32[]{:T(128)}, f32[10,16,64,256]{3,2,1,0:T(8,128)}, bf16[10,64,16,48]{1,3,2,0:T(8,128)(2,1)S(1)}, ...), condition=%wide.region_3.4_spmd, body=%wide.region_2.3_spmd.sunk | while | flops 25952256 | bytes 2164293 | solution.py:99
  90.2 2.4 fusion.136
  92.6 2.3 fusion.136
  99.5 2.4 fusion.136
  101.9 2.4 fusion.136
  104.3 2.4 fusion.136
  106.6 2.4 fusion.136
  111.3 5.5 %reduce_max.18 = bf16[10,16,64]{2,1,0:T(8,128)(2,1)S(1)} reduce(f32[10,16,64,256]{3,2,1,0:T(8,128)} %get-tuple-element.232, bf16[]{:T(256)} %constant.169), dimensions={3}, to_apply=%region_4.5 | reduce | flops 2611200 | bytes 10506242 | tf_op jit(solution)/shard_map/reduce_max | solution.py:100
  116.8 37.0 %pmax.7 = bf16[10,16,64]{2,1,0:T(8,128)(2,1)S(1)} all-reduce(bf16[10,16,64]{2,1,0:T(8,128)(2,1)S(1)} %reduce_max.18), channel_id=1, replica_groups=mesh['row'=32,'col'=8] {'col'}, use_global_device_ids=true, to_apply=%region_5.6 | all-reduce | flops 10240 | bytes 40960 | tf_op jit(solution)/shard_map/pmax | solution.py:114
  153.8 6.4 %copy.91 = bf16[10,256,768]{1,2,0:T(8,128)(2,1)} copy(bf16[10,256,768]{2,1,0:T(8,128)(2,1)} %all-gather.3.cloned.1.call-done) | data formatting | bytes 7864320 | tf_op jit(solution)/shard_map/all_gather | solution.py:85
  160.2 35.6 %while.23 = (s32[]{:T(128)}, bf16[10,64,768]{2,1,0:T(8,128)(2,1)S(1)}, bf16[10,16,64]{2,1,0:T(8,128)(2,1)S(1)}, bf16[10,256,16,48]{1,3,2,0:T(8,128)(2,1)}, f32[1...) while((s32[]{:T(128)}, bf16[10,64,768]{2,1,0:T(8,128)(2,1)S(1)}, ...), condition=%wide.region_8.9_spmd, body=%wide.region_6.8_spmd.sunk | while | flops 26213376 | bytes 3009629 | solution.py:115
  198.7 74.0 %reduce-scatter.5.cloned.1.call-done = bf16[10,16,8]{1,0,2:T(8,128)(2,1)} async-done(((bf16[10,16,64]{1,0,2:T(8,128)(2,1)}), bf16[10,16,8]{1,0,2:T(8,128)(2,1)}) %reduce-scatter.5.cloned.1.call-update) | async-done | bytes 2576 | tf_op jit(solution)/shard_map/reduce_scatter | solution.py:120
  274.0 81.7 %reduce-scatter.3.cloned.1.call-done = bf16[10,8,768]{2,0,1:T(8,128)(2,1)} async-done(((bf16[10,64,768]{2,0,1:T(8,128)(2,1)}), bf16[10,8,768]{2,0,1:T(8,128)(2,1)}) %reduce-scatter.3.cloned.1.call-update) | async-done | bytes 122896 | tf_op jit(solution)/shard_map/reduce_scatter | solution.py:117
  355.7 2.4 fusion.55
  358.3 4.2 %collective-permute-start = (bf16[10,8,128]{2,1,0:T(8,128)(2,1)S(1)}, bf16[10,8,128]{2,1,0:T(8,128)(2,1)S(1)}, u32[]{:S(2)}, u32[]{:S(2)}) collective-permute-start(bf16[10,8,128]{2,1,0:T(8,128)(2,1)S(1)} %convolution_convert_fusion.5), channel_id=1, source_target_pairs={{0,1},{1,2},{2,3},{3,4},{4,5},{5,6},{6,7},{7,8},{8,9},{9,10},{10,1... | collective-permute-start | bytes 61448 | tf_op jit(solution)/shard_map/ppermute | solution.py:18
  366.3 7.8 %collective-permute-start.1 = (bf16[10,48,256]{2,1,0:T(8,128)(2,1)}, bf16[10,48,256]{2,1,0:T(8,128)(2,1)S(1)}, u32[]{:S(2)}, u32[]{:S(2)}) collective-permute-start(bf16[10,48,256]{2,1,0:T(8,128)(2,1)} %copy.107), channel_id=1, source_target_pairs={{0,1},{1,2},{2,3},{3,4},{4,5},{5,6},{6,7},{7,8},{8,9},{9,10},{10,1... | collective-permute-start | bytes 737288 | tf_op jit(solution)/shard_map/ppermute | solution.py:28
  378.8 7.4 %collective-permute-done.2 = bf16[10,48,256]{2,1,0:T(8,128)(2,1)} collective-permute-done((bf16[10,48,256]{2,1,0:T(8,128)(2,1)S(1)}, bf16[10,48,256]{2,1,0:T(8,128)(2,1)}, u32[]{:S(2)}, u32[]{:S(2)}) %collective-permute-start.2) | collective-permute-done | bytes 245792 | tf_op jit(solution)/shard_map/ppermute | solution.py:29
  395.5 4.1 copy.116
  399.7 2.7 reshape.172
  406.1 6.5 %collective-permute-done.3 = bf16[10,8,128]{2,1,0:T(8,128)(2,1)S(1)} collective-permute-done((bf16[10,8,128]{2,1,0:T(8,128)(2,1)S(1)}, bf16[10,8,128]{2,1,0:T(8,128)(2,1)S(1)}, u32[]{:S(2)}, u32[]{:S(2)}) %collective-permute-start.3) | collective-permute-done | bytes 20512 | tf_op jit(solution)/shard_map/ppermute | solution.py:18
  (172 shorter events, 81.8 us)
Async XLA Ops:
  7.2 6.8 %copy-start.2 = (bf16[10,8,768]{2,1,0:T(8,128)(2,1)S(1)}, bf16[10,8,768]{2,1,0:T(8,128)(2,1)}, u32[]{:S(2)}) copy-start(bf16[10,8,768]{2,1,0:T(8,128)(2,1)} %param.24) | copy-start | bytes 368644
  7.2 6.8 %copy-start.11 = (f32[768]{0:T(1024)S(1)}, f32[768]{0:T(1024)}, u32[]{:S(2)}) copy-start(f32[768]{0:T(1024)} %param.26) | copy-start | bytes 9220
  7.2 6.8 %copy-start.4 = (bf16[768,768]{1,0:T(8,128)(2,1)S(1)}, bf16[768,768]{1,0:T(8,128)(2,1)}, u32[]{:S(2)}) copy-start(bf16[768,768]{1,0:T(8,128)(2,1)} %param.27) | copy-start | bytes 3538948
  7.2 74.4 %all-gather.5.cloned.1.call-start = ((), (), s32[]{:S(2)}) async-start(), calls=%async_computation.3 | async-start | bytes 4055040 | tf_op jit(solution)/shard_map/all_gather | solution.py:84
  11.5 142.3 %all-gather.3.cloned.1.call-start = ((), (), s32[]{:S(2)}) async-start(), calls=%async_computation.2 | async-start | bytes 4055040 | tf_op jit(solution)/shard_map/all_gather | solution.py:85
  13.9 258.7 %reduce-scatter.5.cloned.1.call-start = ((), (), s32[]{:S(2)}) async-start(), calls=%async_computation.5 | async-start | bytes 294912 | tf_op jit(solution)/shard_map/reduce_scatter | solution.py:120
  153.8 6.4 %copy-start.5 = (bf16[10,64,768]{2,1,0:T(8,128)(2,1)S(1)}, bf16[10,64,768]{2,1,0:T(8,128)(2,1)}, u32[]{:S(2)}) copy-start(bf16[10,64,768]{2,1,0:T(8,128)(2,1)} %custom-call.1) | copy-start | bytes 2949124
  196.7 159.0 %reduce-scatter.3.cloned.1.call-start = ((), (), s32[]{:S(2)}) async-start(), calls=%async_computation.4 | async-start | bytes 1769472 | tf_op jit(solution)/shard_map/reduce_scatter | solution.py:117
  273.9 84.1 %copy-start.8 = (bf16[768,128]{1,0:T(8,128)(2,1)S(1)}, bf16[768,128]{1,0:T(8,128)(2,1)}, u32[]{:S(2)}) copy-start(bf16[768,128]{1,0:T(8,128)(2,1)} %param.32) | copy-start | bytes 589828
  274.0 88.6 %copy-start.19 = (s32[128]{0:T(128)S(1)}, s32[128]{0:T(128)}, u32[]{:S(2)}) copy-start(s32[128]{0:T(128)} %param.34) | copy-start | bytes 1540
  274.0 88.6 %copy-start.6 = (bf16[10,128,128]{2,1,0:T(8,128)(2,1)S(1)}, bf16[10,128,128]{2,1,0:T(8,128)(2,1)}, u32[]{:S(2)}) copy-start(bf16[10,128,128]{2,1,0:T(8,128)(2,1)} %param.33) | copy-start | bytes 983044
  358.1 4.5 %copy-start.10 = (bf16[10,8,768]{2,1,0:T(8,128)(2,1)}, bf16[10,8,768]{2,1,0:T(8,128)(2,1)S(1)}, u32[]{:S(2)}) copy-start(bf16[10,8,768]{2,1,0:T(8,128)(2,1)S(1)} %fusion.55) | copy-start | bytes 368644
  358.1 6.3 %copy-start.12 = (bf16[128,128]{1,0:T(8,128)(2,1)S(1)}, bf16[128,128]{1,0:T(8,128)(2,1)}, u32[]{:S(2)}) copy-start(bf16[128,128]{1,0:T(8,128)(2,1)} %param.38) | copy-start | bytes 98308
  358.1 6.3 %copy-start.15 = (f32[128]{0:T(128)S(1)}, f32[128]{0:T(128)}, u32[]{:S(2)}) copy-start(f32[128]{0:T(128)} %param.36) | copy-start | bytes 1540
  358.1 6.6 %copy-start.13 = (bf16[128,128]{1,0:T(8,128)(2,1)S(1)}, bf16[128,128]{1,0:T(8,128)(2,1)}, u32[]{:S(2)}) copy-start(bf16[128,128]{1,0:T(8,128)(2,1)} %param.39) | copy-start | bytes 98308
  358.3 5.7 %collective-permute-start = (bf16[10,8,128]{2,1,0:T(8,128)(2,1)S(1)}, bf16[10,8,128]{2,1,0:T(8,128)(2,1)S(1)}, u32[]{:S(2)}, u32[]{:S(2)}) collective-permute-start(bf16[10,8,128]{2,1,0:T(8,128)(2,1)S(1)} %convolution_convert_fusion.5), channel_id=1, source_target_pairs={{0,1},{1,2},{2,3},{3,4},{4,5},{5,6},{6,7},{7,8},{8,9},{9,10},{10,1... | collective-permute-start | bytes 61448 | tf_op jit(solution)/shard_map/ppermute | solution.py:18
  365.1 11.4 %copy-start.14 = (bf16[128,128]{1,0:T(8,128)(2,1)S(1)}, bf16[128,128]{1,0:T(8,128)(2,1)}, u32[]{:S(2)}) copy-start(bf16[128,128]{1,0:T(8,128)(2,1)} %param.37) | copy-start | bytes 98308
  366.3 12.1 %collective-permute-start.1 = (bf16[10,48,256]{2,1,0:T(8,128)(2,1)}, bf16[10,48,256]{2,1,0:T(8,128)(2,1)S(1)}, u32[]{:S(2)}, u32[]{:S(2)}) collective-permute-start(bf16[10,48,256]{2,1,0:T(8,128)(2,1)} %copy.107), channel_id=1, source_target_pairs={{0,1},{1,2},{2,3},{3,4},{4,5},{5,6},{6,7},{7,8},{8,9},{9,10},{10,1... | collective-permute-start | bytes 737288 | tf_op jit(solution)/shard_map/ppermute | solution.py:28
  374.4 11.8 %collective-permute-start.2 = (bf16[10,48,256]{2,1,0:T(8,128)(2,1)S(1)}, bf16[10,48,256]{2,1,0:T(8,128)(2,1)}, u32[]{:S(2)}, u32[]{:S(2)}) collective-permute-start(bf16[10,48,256]{2,1,0:T(8,128)(2,1)S(1)} %copy.109), channel_id=1, source_target_pairs={{1,0},{2,1},{3,2},{4,3},{5,4},{6,5},{7,6},{8,7},{9,8},{10,9},{11,1... | collective-permute-start | bytes 737288 | tf_op jit(solution)/shard_map/ppermute | solution.py:29
  399.7 2.7 copy-start.18
  399.7 14.1 %copy-start.1 = (bf16[768,768]{1,0:T(8,128)(2,1)S(1)}, bf16[768,768]{1,0:T(8,128)(2,1)}, u32[]{:S(2)}) copy-start(bf16[768,768]{1,0:T(8,128)(2,1)} %param.28) | copy-start | bytes 3538948
  402.4 10.4 %copy-start.7 = (bf16[128,768]{1,0:T(8,128)(2,1)S(1)}, bf16[128,768]{1,0:T(8,128)(2,1)}, u32[]{:S(2)}) copy-start(bf16[128,768]{1,0:T(8,128)(2,1)} %param.43) | copy-start | bytes 589828
  402.4 10.4 %copy-start.16 = (f32[128]{0:T(128)S(1)}, f32[128]{0:T(128)}, u32[]{:S(2)}) copy-start(f32[128]{0:T(128)} %param.42) | copy-start | bytes 1540
  403.2 9.3 %collective-permute-start.3 = (bf16[10,8,128]{2,1,0:T(8,128)(2,1)S(1)}, bf16[10,8,128]{2,1,0:T(8,128)(2,1)S(1)}, u32[]{:S(2)}, u32[]{:S(2)}) collective-permute-start(bf16[10,8,128]{2,1,0:T(8,128)(2,1)S(1)} %slice.70), channel_id=1, source_target_pairs={{1,0},{2,1},{3,2},{4,3},{5,4},{6,5},{7,6},{8,7},{9,8},{10,9},{11,1... | collective-permute-start | bytes 61448 | tf_op jit(solution)/shard_map/ppermute | solution.py:18
  (4 other events, 8.3 us)
Sparse Core Ops, SparseCore 0:
  11.6 69.9 all-gather.4
  83.9 66.5 all-gather.2
  196.9 75.7 reduce-scatter.4
  277.1 78.5 reduce-scatter.2
where the time goes:
time: 426 us; the launch traced here: 420 us
  waiting for transfers between devices  196 us (46%)
  blocking collectives  73.3 us (17%)
  matrix products  54.1 us (13%)
  local copies, waits for them, and re-layouts  37.9 us (9%)
  other arithmetic  28.3 us (7%)
  starting transfers between devices  16.2 us (4%)
  between operations  14.4 us (3%)
    reduce_scatter x1, waiting for transfers between devices, on_device(): lax.psum_scatter(mixed_all.astype(jnp.bfloat16), 'col', scatter_dimension...  81.7 us
    reduce_scatter x1, waiting for transfers between devices, on_device(): lax.psum_scatter(totals_all.astype(jnp.bfloat16), 'col', scatter_dimensio...  74 us
    pmax x1, blocking collectives, on_device(): lax.pmax(tile_max.astype(jnp.bfloat16), 'col').astype(tile_max.dtype)  37 us
    all_gather x1, blocking collectives, on_device(): query_block = lax.all_gather(query, 'col', axis=1, tiled=True)  36.3 us
    all_gather x1, waiting for transfers between devices, on_device(): lax.all_gather(key_part, 'row', axis=1, tiled=True)  24.8 us
    dot_general x10, matrix products, score_one(): jnp.einsum('qhd,khd->hqk', query_one, key_one, preferred_element_type=jnp...  23.5 us
    dot_general x10, matrix products, weigh_one(): jnp.einsum('hqk,khd->qhd', weights.astype(jnp.bfloat16), value_one, prefe...  17.2 us
    reduce_sum x10, other arithmetic, weigh_one(): totals = jnp.sum(weights, axis=-1)  16.3 us
  transfers between devices with their start and end apart: 8, of which 6 were waited for; matrix products, arithmetic and copies ran while one was open for 12% of the time, Pallas kernels for 0%

commit v1 on v0

--- a/solution.py
+++ b/solution.py
@@ -1,9 +1,15 @@
+import functools
 import math
 
 import jax
 import jax.numpy as jnp
 from jax import lax
+from jax.experimental import pallas as pl
+from jax.experimental.pallas import tpu as pltpu
 from jax.sharding import PartitionSpec as P
+
+MESH = pl.DeviceIdType.MESH
+LANES = 128
 
 WQ = 32
 WK = 128
@@ -42,6 +48,530 @@
     flat = inputs.reshape(-1, inputs.shape[-1])
     result = jnp.dot(flat, weight, preferred_element_type=jnp.float32)
     return result.reshape(inputs.shape[:-1] + (weight.shape[1],))
+
+
+def lane_index(shape):
+    return lax.broadcasted_iota(jnp.int32, shape, len(shape) - 1)
+
+
+def roll_left(values, amount):
+    width = values.shape[-1]
+    amount = amount % width
+    if amount == 0:
+        return values
+    return pltpu.roll(values, width - amount, values.ndim - 1)
+
+
+def window(values, start, count):
+    tile, rest = divmod(start, LANES)
+    if rest + count <= LANES:
+        return roll_left(values[:, tile * LANES : (tile + 1) * LANES], rest)
+    return roll_left(values[:, tile * LANES : (tile + 2) * LANES], rest)[:, :LANES]
+
+
+def token_kernel(
+    heads,
+    rows_plane,
+    planes,
+    n_col,
+    x_ref,
+    gain_ref,
+    bias_hbm,
+    wq_hbm,
+    wk_hbm,
+    wv_hbm,
+    wg_hbm,
+    wo_hbm,
+    wc_hbm,
+    update_ref,
+    cond_ref,
+    bias_in,
+    wq,
+    wk,
+    wv,
+    wg,
+    wo,
+    wc,
+    bias_f,
+    bias_t,
+    bias_send,
+    bias_recv,
+    bias_keys,
+    bias_all,
+    kv_send,
+    kv_recv,
+    q_send,
+    q_recv,
+    kv_ring,
+    q_all,
+    scores,
+    out_f,
+    oa_send,
+    oa_recv,
+    ob_send,
+    ob_recv,
+    gate_s,
+    load_sem,
+    a2a_send_sem,
+    a2a_recv_sem,
+    ring_send_sem,
+    ring_recv_sem,
+):
+    samples, tokens, width = x_ref.shape
+    head_dim = width // heads
+    per_core = samples // 2
+    half_ring = planes // 2
+    peers = rows_plane * n_col
+    flat = samples * tokens
+    part = per_core * tokens
+    queries = tokens * n_col
+    plane_tokens = peers * tokens
+
+    row, col = lax.axis_index("row"), lax.axis_index("col")
+    z, r4 = row // rows_plane, row % rows_plane
+    me = r4 * n_col + col
+    my_core = r4 % 2
+    my_head = (r4 // 2) * n_col + col
+
+    def device_of(p):
+        return (z * rows_plane + p // n_col, p % n_col)
+
+    def head_of(p):
+        return (p // n_col) // 2 * n_col + p % n_col, (p // n_col) % 2
+
+    def ring_device(step):
+        other = lax.rem(z + step + planes, planes)
+        return (other * rows_plane + r4, col)
+
+    loads = [
+        pltpu.make_async_copy(source, target, load_sem.at[i])
+        for i, (source, target) in enumerate(
+            (
+                (bias_hbm, bias_in),
+                (wk_hbm, wk),
+                (wv_hbm, wv),
+                (wq_hbm, wq),
+                (wg_hbm, wg),
+                (wo_hbm, wo),
+                (wc_hbm, wc),
+            )
+        )
+    ]
+    for load in loads:
+        load.start()
+
+    barrier = pltpu.get_barrier_semaphore()
+
+    def greet(i, carry):
+        pl.semaphore_signal(
+            barrier, inc=1, device_id=device_of(lax.rem(me + i, peers)), device_id_type=MESH
+        )
+        return carry
+
+    lax.fori_loop(1, peers, greet, 0)
+    for step in (1, -1):
+        pl.semaphore_signal(barrier, inc=1, device_id=ring_device(step), device_id_type=MESH)
+
+    loads[0].wait()
+    columns = bias_in.shape[2]
+    flat_bias = bias_in[...].astype(jnp.float32).reshape(queries * tokens, columns)
+    for tile in range(columns // LANES):
+        bias_f[tile] = flat_bias[:, tile * LANES : (tile + 1) * LANES]
+    rho = lax.broadcasted_iota(jnp.int32, (columns, columns), 0)
+    lam = lane_index((columns, columns))
+    ylo, rest = rho // (columns // 2), rho % (columns // 2)
+    hd, rest = rest // (planes * 2), rest % (planes * 2)
+    pz, core = rest // 2, rest % 2
+    source = ((pz * 2 + ylo) * 2 + core) * heads + hd
+    order = (lam == source).astype(jnp.bfloat16)
+    low = lane_index((columns // 2, LANES)) < queries
+    for j in range(tokens // 2):
+        two = jnp.concatenate(
+            [
+                jnp.concatenate(
+                    [
+                        bias_f[tile, pl.ds(j + jj * (tokens // 2), queries, stride=tokens), :]
+                        for tile in range(columns // LANES)
+                    ],
+                    axis=1,
+                )
+                for jj in range(2)
+            ],
+            axis=0,
+        ).astype(jnp.bfloat16)
+        moved = lax.dot_general(
+            order, two, (((1,), (1,)), ((), ())), preferred_element_type=jnp.float32
+        )
+        top, bottom = moved[: columns // 2], moved[columns // 2 :]
+        bias_t[pl.ds(j, columns // 2, stride=tokens), :] = jnp.where(
+            low, top, pltpu.roll(bottom, queries, 1)
+        )
+        bias_t[pl.ds(j + tokens // 2, columns // 2, stride=tokens), :] = jnp.where(
+            low, pltpu.roll(top, queries, 1), bottom
+        )
+    piece = planes * 2 * tokens
+    bias_send[...] = bias_t[...].astype(jnp.bfloat16).reshape(heads, piece, LANES)
+
+    pl.semaphore_wait(barrier, peers + 1)
+
+    def send_bias(i, carry):
+        p = lax.rem(me + i, peers)
+        head, _ = head_of(p)
+        pltpu.make_async_remote_copy(
+            src_ref=bias_send.at[head],
+            dst_ref=bias_recv.at[me],
+            send_sem=a2a_send_sem.at[0],
+            recv_sem=a2a_recv_sem.at[0],
+            device_id=device_of(p),
+            device_id_type=MESH,
+        ).start()
+        return carry
+
+    lax.fori_loop(1, peers, send_bias, 0)
+    bias_recv[me] = bias_send[my_head]
+
+    values = x_ref[...].astype(jnp.float32).reshape(flat, width)
+    center = values - jnp.mean(values, axis=-1, keepdims=True)
+    spread = jnp.mean(center * center, axis=-1, keepdims=True)
+    normed = (center * lax.rsqrt(spread + EPSILON) * gain_ref[...]).astype(jnp.bfloat16)
+
+    loads[1].wait()
+    key = jnp.dot(normed, wk[...], preferred_element_type=jnp.float32)
+    loads[2].wait()
+    value = jnp.dot(normed, wv[...], preferred_element_type=jnp.float32)
+    first = lane_index((flat, LANES)) < head_dim
+    second = lane_index((flat, LANES)) < 2 * head_dim
+    pad_rows = kv_send.shape[2] - part
+    zero_rows = jnp.zeros((pad_rows, LANES), jnp.float32)
+    for head in range(heads):
+        k_part = window(key, head * head_dim, head_dim)
+        v_part = window(value, head * head_dim, head_dim)
+        both = jnp.where(
+            first, k_part, jnp.where(second, pltpu.roll(v_part, head_dim, 1), 0.0)
+        )
+        for core in range(2):
+            kv_send[core, head] = jnp.concatenate(
+                [both[core * part : (core + 1) * part], zero_rows], axis=0
+            ).astype(jnp.bfloat16)
+
+    my_slot = col * rows_plane + r4
+
+    def send_kv(i, carry):
+        p = lax.rem(me + i, peers)
+        head, core = head_of(p)
+        pltpu.make_async_remote_copy(
+            src_ref=kv_send.at[core, head],
+            dst_ref=kv_recv.at[my_slot],
+            send_sem=a2a_send_sem.at[1],
+            recv_sem=a2a_recv_sem.at[1],
+            device_id=device_of(p),
+            device_id_type=MESH,
+        ).start()
+        return carry
+
+    lax.fori_loop(1, peers, send_kv, 0)
+    kv_recv[my_slot] = kv_send[my_core, my_head]
+
+    loads[3].wait()
+    query = jnp.dot(normed, wq[...], preferred_element_type=jnp.float32)
+    for head in range(heads):
+        q_part = jnp.where(first, window(query, head * head_dim, head_dim), 0.0)
+        for core in range(2):
+            q_send[core, head] = jnp.concatenate(
+                [q_part[core * part : (core + 1) * part], zero_rows], axis=0
+            ).astype(jnp.bfloat16)
+
+    def send_q(i, carry):
+        p = lax.rem(me + i, peers)
+        head, core = head_of(p)
+        pltpu.make_async_remote_copy(
+            src_ref=q_send.at[core, head],
+            dst_ref=q_recv.at[me],
+            send_sem=a2a_send_sem.at[2],
+            recv_sem=a2a_recv_sem.at[2],
+            device_id=device_of(p),
+            device_id_type=MESH,
+        ).start()
+        return carry
+
+    lax.fori_loop(1, peers, send_q, 0)
+    q_recv[me] = q_send[my_core, my_head]
+
+    loads[4].wait()
+    gate_s[...] = jnp.dot(normed, wg[...], preferred_element_type=jnp.float32).astype(jnp.bfloat16)
+
+    def wait_all(buffer, sem):
+        view = buffer.at[pl.ds(0, peers - 1)]
+        pltpu.make_async_copy(view, view, sem).wait()
+
+    wait_all(kv_recv, a2a_recv_sem.at[1])
+    kv_all = kv_recv[...].astype(jnp.float32)
+    eye_rows = lax.broadcasted_iota(jnp.int32, (2 * head_dim, LANES), 0)
+    eye = (eye_rows == lane_index((2 * head_dim, LANES))).astype(jnp.bfloat16)
+    for s in range(per_core):
+        rows = kv_all[:, s * tokens : (s + 1) * tokens, :].reshape(plane_tokens, LANES)
+        kv_ring[z, s] = lax.dot_general(
+            eye,
+            rows.astype(jnp.bfloat16),
+            (((1,), (1,)), ((), ())),
+            preferred_element_type=jnp.float32,
+        ).astype(jnp.bfloat16)
+
+    def ring_block(way, hop, s):
+        back = -hop if way == 0 else hop
+        block = lax.rem(z + back + planes, planes)
+        if hop < half_ring:
+            return kv_ring.at[block, s]
+        return kv_ring.at[block, s, pl.ds(way * head_dim, head_dim)]
+
+    def ring_send(way, hop, s):
+        back = 1 - hop if way == 0 else hop - 1
+        block = lax.rem(z + back + planes, planes)
+        view = kv_ring.at[block, s]
+        if hop == half_ring:
+            view = kv_ring.at[block, s, pl.ds(way * head_dim, head_dim)]
+        return pltpu.make_async_remote_copy(
+            src_ref=view,
+            dst_ref=view,
+            send_sem=ring_send_sem.at[way, hop - 1, s],
+            recv_sem=ring_recv_sem.at[way, hop - 1, s],
+            device_id=ring_device(1 if way == 0 else -1),
+            device_id_type=MESH,
+        )
+
+    def ring_wait(way, hop, s):
+        view = ring_block(way, hop, s)
+        pltpu.make_async_copy(view, view, ring_recv_sem.at[way, hop - 1, s]).wait()
+
+    log2e = math.log2(math.e)
+    factor = log2e / math.sqrt(head_dim)
+
+    def bias_stage():
+        wait_all(bias_recv, a2a_recv_sem.at[0])
+        half_lanes = lane_index((piece, LANES)) < queries
+        for c in range(n_col):
+            for pair in range(rows_plane // 2):
+                even = bias_recv[(2 * pair) * n_col + c].astype(jnp.float32)
+                odd = bias_recv[(2 * pair + 1) * n_col + c].astype(jnp.float32)
+                for y, merged in enumerate(
+                    (
+                        jnp.where(half_lanes, even, pltpu.roll(odd, queries, 1)),
+                        jnp.where(half_lanes, pltpu.roll(even, queries, 1), odd),
+                    )
+                ):
+                    bias_keys[:, c, y, :, pair * LANES : (pair + 1) * LANES] = merged.astype(
+                        jnp.bfloat16
+                    ).reshape(planes, 2 * tokens, LANES)
+        eye_row = lax.broadcasted_iota(jnp.int32, (plane_tokens, plane_tokens), 0)
+        eye_q = (eye_row == lane_index((plane_tokens, plane_tokens))).astype(jnp.bfloat16)
+        for zz in range(planes):
+            block = bias_keys[zz].reshape(plane_tokens, plane_tokens)
+            bias_all[zz] = (
+                lax.dot_general(
+                    eye_q, block, (((1,), (1,)), ((), ())), preferred_element_type=jnp.float32
+                )
+                * log2e
+            )
+        wait_all(q_recv, a2a_recv_sem.at[2])
+        q_rows = q_recv[...].astype(jnp.float32)
+        for s in range(per_core):
+            q_all[s] = (
+                q_rows[:, s * tokens : (s + 1) * tokens, :]
+                .reshape(plane_tokens, LANES)
+                .astype(jnp.bfloat16)
+            )
+
+    def attend(s):
+        q_one = q_all[s][:, :head_dim]
+        peak = None
+        for zz in range(planes):
+            raw = jnp.dot(q_one, kv_ring[zz, s, :head_dim, :], preferred_element_type=jnp.float32)
+            score = raw * factor + bias_all[zz]
+            scores[zz] = score
+            peak = score if peak is None else jnp.maximum(peak, score)
+        peak = jnp.max(peak, axis=-1, keepdims=True)
+        total = None
+        ones = jnp.ones((LANES - head_dim, plane_tokens), jnp.bfloat16)
+        for zz in range(planes):
+            weights = jnp.exp2(scores[zz] - peak).astype(jnp.bfloat16)
+            v_one = jnp.concatenate([kv_ring[zz, s, head_dim:, :], ones], axis=0)
+            mixed = lax.dot_general(
+                weights, v_one, (((1,), (1,)), ((), ())), preferred_element_type=jnp.float32
+            )
+            total = mixed if total is None else total + mixed
+        attended = total / total[:, head_dim : head_dim + 1]
+        out_f[s] = attended.reshape(peers, tokens, LANES)
+
+    def send_out(buffer, target, which):
+        def body(i, carry):
+            p = lax.rem(me + i, peers)
+            pltpu.make_async_remote_copy(
+                src_ref=buffer.at[p],
+                dst_ref=target.at[my_core * heads + my_head],
+                send_sem=a2a_send_sem.at[which],
+                recv_sem=a2a_recv_sem.at[which],
+                device_id=device_of(p),
+                device_id_type=MESH,
+            ).start()
+            return carry
+
+        lax.fori_loop(1, peers, body, 0)
+        target[my_core * heads + my_head] = buffer[me]
+
+    def step(k, carry):
+        @pl.when(k < per_core)
+        def _():
+            for way in range(2):
+                ring_send(way, 1, k).start()
+
+        for hop in range(1, half_ring + 1):
+            s = k - hop
+
+            @pl.when((s >= 0) & (s < per_core))
+            def _(hop=hop, s=s):
+                for way in range(2):
+                    ring_wait(way, hop, s)
+                    if hop < half_ring:
+                        ring_send(way, hop + 1, s).start()
+
+        @pl.when(k == half_ring - 1)
+        def _():
+            bias_stage()
+
+        @pl.when(k >= half_ring)
+        def _():
+            attend(k - half_ring)
+
+        @pl.when(k == half_ring + per_core - 2)
+        def _():
+            oa_send[...] = jnp.concatenate(
+                [out_f[s] for s in range(per_core - 1)], axis=1
+            ).astype(jnp.bfloat16)
+            send_out(oa_send, oa_recv, 3)
+
+        return carry
+
+    lax.fori_loop(0, per_core + half_ring, step, 0)
+    last = out_f[per_core - 1]
+    ob_send[...] = jnp.concatenate([last, jnp.zeros_like(last)], axis=1).astype(jnp.bfloat16)
+    send_out(ob_send, ob_recv, 4)
+
+    wait_all(oa_recv, a2a_recv_sem.at[3])
+    wait_all(ob_recv, a2a_recv_sem.at[4])
+    tiles = [None] * (width // LANES)
+    lanes = lane_index((flat, LANES))
+    for head in range(heads):
+        piece_rows = jnp.concatenate(
+            [
+                part_rows
+                for core in range(2)
+                for part_rows in (
+                    oa_recv[core * heads + head].astype(jnp.float32),
+                    ob_recv[core * heads + head].astype(jnp.float32)[:tokens],
+                )
+            ],
+            axis=0,
+        )
+        tile, rest = divmod(head * head_dim, LANES)
+        moved = pltpu.roll(piece_rows, rest, 1) if rest else piece_rows
+        tiles[tile] = moved if tiles[tile] is None else jnp.where(lanes >= rest, moved, tiles[tile])
+        if rest + head_dim > LANES:
+            tiles[tile + 1] = moved
+    attended = jnp.concatenate(tiles, axis=1)
+    gated = (attended * jax.nn.sigmoid(gate_s[...].astype(jnp.float32))).astype(jnp.bfloat16)
+    loads[5].wait()
+    update = jnp.dot(gated, wo[...], preferred_element_type=jnp.float32)
+    update_ref[...] = update.reshape(samples, tokens, width).astype(jnp.bfloat16)
+    loads[6].wait()
+    cond = jnp.dot(update.astype(jnp.bfloat16), wc[...], preferred_element_type=jnp.float32)
+    cond_ref[...] = cond.reshape(samples, tokens, cond.shape[-1]).astype(jnp.bfloat16)
+
+    for which, buffer in ((0, bias_recv), (1, kv_recv), (2, q_recv), (3, oa_recv), (4, ob_recv)):
+        wait_all(buffer, a2a_send_sem.at[which])
+
+    def drain(s, carry):
+        for way in range(2):
+            for hop in range(1, half_ring + 1):
+                ring_send(way, hop, s).wait_send()
+        return carry
+
+    lax.fori_loop(0, per_core, drain, 0)
+
+
+def token_stage(
+    single, pair_bias, token_gain, w_query, w_key, w_value, w_gate, w_out, w_cond, n_row, n_col
+):
+    samples, tokens, width = single.shape
+    queries, _, columns = pair_bias.shape
+    heads = columns // n_row
+    head_dim = width // heads
+    rows_plane = 2 * heads // n_col
+    planes = n_row // rows_plane
+    peers = rows_plane * n_col
+    per_core = samples // 2
+    plane_tokens = peers * tokens
+    padded = -(-per_core * tokens // 16) * 16
+    piece = planes * 2 * tokens
+    cond_width = w_cond.shape[1]
+    early = (per_core - 1) * tokens
+    bf16, f32 = jnp.bfloat16, jnp.float32
+    vmem = pl.BlockSpec(memory_space=pltpu.VMEM)
+    anywhere = pl.BlockSpec(memory_space=pl.ANY)
+    return pl.pallas_call(
+        functools.partial(token_kernel, heads, rows_plane, planes, n_col),
+        out_shape=(
+            jax.ShapeDtypeStruct((samples, tokens, width), bf16),
+            jax.ShapeDtypeStruct((samples, tokens, cond_width), bf16),
+        ),
+        in_specs=[vmem, vmem] + [anywhere] * 7,
+        out_specs=(vmem, vmem),
+        scratch_shapes=[
+            pltpu.VMEM(pair_bias.shape, bf16),
+            pltpu.VMEM(w_query.shape, bf16),
+            pltpu.VMEM(w_key.shape, bf16),
+            pltpu.VMEM(w_value.shape, bf16),
+            pltpu.VMEM(w_gate.shape, bf16),
+            pltpu.VMEM(w_out.shape, bf16),
+            pltpu.VMEM(w_cond.shape, bf16),
+            pltpu.VMEM((columns // LANES, queries * tokens, LANES), f32),
+            pltpu.VMEM((heads * piece, LANES), f32),
+            pltpu.VMEM((heads, piece, LANES), bf16),
+            pltpu.VMEM((peers, piece, LANES), bf16),
+            pltpu.VMEM((planes, n_col, 2, 2 * tokens, plane_tokens), bf16),
+            pltpu.VMEM((planes, plane_tokens, plane_tokens), f32),
+            pltpu.VMEM((2, heads, padded, LANES), bf16),
+            pltpu.VMEM((peers, padded, LANES), bf16),
+            pltpu.VMEM((2, heads, padded, LANES), bf16),
+            pltpu.VMEM((peers, padded, LANES), bf16),
+            pltpu.VMEM((planes, per_core, 2 * head_dim, plane_tokens), bf16),
+            pltpu.VMEM((per_core, plane_tokens, LANES), bf16),
+            pltpu.VMEM((planes, plane_tokens, plane_tokens), f32),
+            pltpu.VMEM((per_core, peers, tokens, LANES), f32),
+            pltpu.VMEM((peers, early, LANES), bf16),
+            pltpu.VMEM((peers, early, LANES), bf16),
+            pltpu.VMEM((peers, 2 * tokens, LANES), bf16),
+            pltpu.VMEM((peers, 2 * tokens, LANES), bf16),
+            pltpu.VMEM((samples * tokens, width), bf16),
+            pltpu.SemaphoreType.DMA((7,)),
+            pltpu.SemaphoreType.DMA((5,)),
+            pltpu.SemaphoreType.DMA((5,)),
+            pltpu.SemaphoreType.DMA((2, planes // 2, per_core)),
+            pltpu.SemaphoreType.DMA((2, planes // 2, per_core)),
+        ],
+        compiler_params=pltpu.CompilerParams(
+            collective_id=1, has_side_effects=True, vmem_limit_bytes=56 * 1024 * 1024
+        ),
+    )(
+        single,
+        token_gain.reshape(1, width),
+        pair_bias,
+        w_query,
+        w_key,
+        w_value,
+        w_gate,
+        w_out,
+        w_cond,
+    )
 
 
 def on_device(
@@ -69,66 +599,9 @@
     n_row = lax.axis_size("row")
     n_col = lax.axis_size("col")
     samples, tok_dev, width = single.shape
-    heads = pair_bias.shape[2] // n_row
-    head_dim = width // heads
-    block_rows = tok_dev * n_col
-    tile_keys = tok_dev * n_row
-    scale = 1.0 / math.sqrt(head_dim)
-    normed = layer_norm(single, token_gain).astype(jnp.bfloat16)
-    query = matmul(normed, w_query).astype(jnp.bfloat16)
-    gate_lin = matmul(normed, w_gate).astype(jnp.bfloat16)
-    query_block = lax.all_gather(query, "col", axis=1, tiled=True)
-    key_part = matmul(normed, w_key).astype(jnp.bfloat16)
-    value_part = matmul(normed, w_value).astype(jnp.bfloat16)
-    key_block, value_block = (
-        lax.all_gather(key_part, "row", axis=1, tiled=True),
-        lax.all_gather(value_part, "row", axis=1, tiled=True),
-    )
-    bias_tile = jnp.transpose(
-        pair_bias.reshape(block_rows, tok_dev, n_row, heads), (3, 0, 2, 1)
-    ).reshape(heads, block_rows, tile_keys)
-    query_heads = query_block.reshape(samples, block_rows, heads, head_dim)
-    key_heads = key_block.reshape(samples, tile_keys, heads, head_dim)
-    value_heads = value_block.reshape(samples, tile_keys, heads, head_dim)
-
-    def score_one(members):
-        query_one, key_one = members
-        raw = jnp.einsum("qhd,khd->hqk", query_one, key_one, preferred_element_type=jnp.float32)
-        return raw * scale + bias_tile.astype(jnp.float32)
-
-    scores = lax.map(score_one, (query_heads, key_heads))
-    tile_max = jnp.max(scores, axis=-1)
-
-    def weigh_one(members):
-        scores_one, maxima_one, value_one = members
-        weights = jnp.exp(scores_one - maxima_one[:, :, None])
-        totals = jnp.sum(weights, axis=-1)
-        mixed = jnp.einsum(
-            "hqk,khd->qhd",
-            weights.astype(jnp.bfloat16),
-            value_one,
-            preferred_element_type=jnp.float32,
-        )
-        return (mixed.reshape(block_rows, width), totals)
-
-    maxima = lax.pmax(tile_max.astype(jnp.bfloat16), "col").astype(tile_max.dtype)
-    mixed_all, totals_all = lax.map(weigh_one, (scores, maxima, value_heads))
-    mixed_own, totals_own = (
-        lax.psum_scatter(
-            mixed_all.astype(jnp.bfloat16), "col", scatter_dimension=1, tiled=True
-        ).astype(jnp.float32),
-        lax.psum_scatter(
-            totals_all.astype(jnp.bfloat16), "col", scatter_dimension=2, tiled=True
-        ).astype(jnp.float32),
-    )
-    attended = (
-        mixed_own.reshape(samples, tok_dev, heads, head_dim)
-        / jnp.transpose(totals_own, (0, 2, 1))[..., None]
-    )
-    attended = attended.reshape(samples, tok_dev, width)
-    gated = (attended * jax.nn.sigmoid(gate_lin.astype(jnp.float32))).astype(jnp.bfloat16)
-    token_update = matmul(gated, w_out).astype(jnp.bfloat16)
-    cond = matmul(token_update, w_cond).astype(jnp.bfloat16)
+    token_update, cond = token_stage(
+        single, pair_bias, token_gain, w_query, w_key, w_value, w_gate, w_out, w_cond, n_row, n_col
+    )
     cond_lower = shifted(cond, ("row", "col"), 1)
     cond_rim = jnp.concatenate([cond_lower, cond], axis=1)
     device = lax.axis_index(("row", "col"))

time: 426 us -> 120 us (0.28)
  waiting for transfers between devices: 196 us -> 10.6 us
  blocking collectives: 73.3 us -> 0 us
  Pallas kernels: 0 us -> 63.9 us
  matrix products: 54.1 us -> 8.04 us
  other arithmetic: 28.3 us -> 3.52 us
  local copies, waits for them, and re-layouts: 37.9 us -> 13.8 us
  between operations: 14.4 us -> 0.98 us
    reduce_scatter x2 -> x0, waiting for transfers between devices: 156 us -> none  [the longest x1 81.7 us: on_device(): lax.psum_scatter(mixed_all.astype(jnp.bfloat16), 'col', scatter_dimension...]
    pallas_call x0 -> x1, Pallas kernels: none -> 63.9 us  [token_stage(): pl.pallas_call(functools.partial(token_kernel, heads, rows_plane, planes,...]
    dot_general x20 -> x0, matrix products: 40.6 us -> none  [the longest x10 23.5 us: score_one(): jnp.einsum('qhd,khd->hqk', query_one, key_one, preferred_element_type=jnp...]
    pmax x1 -> x0, blocking collectives: 37 us -> none  [on_device(): lax.pmax(tile_max.astype(jnp.bfloat16), 'col').astype(tile_max.dtype)]
    all_gather x1 -> x0, blocking collectives: 36.3 us -> none  [on_device(): query_block = lax.all_gather(query, 'col', axis=1, tiled=True)]
    all_gather x2 -> x0, waiting for transfers between devices: 24.9 us -> none  [the longest x1 24.8 us: on_device(): lax.all_gather(key_part, 'row', axis=1, tiled=True)]
    reduce_sum x10 -> x0, other arithmetic: 16.3 us -> none  [weigh_one(): totals = jnp.sum(weights, axis=-1)]
    all_gather x2 -> x0, local copies, waits for them, and re-layouts: 12.6 us -> none  [the longest x1 6.36 us: on_device(): lax.all_gather(value_part, 'row', axis=1, tiled=True)]
  transfers between devices with their start and end apart: 8 -> 4, of which waited for: 6 -> 3; matrix products, arithmetic and copies ran while one was open for 12% -> 3% of each run, Pallas kernels for 0% -> 0%
where the time goes in v1:
time: 120 us; the launch traced here: 118 us
  Pallas kernels  63.9 us (53%)
  starting transfers between devices  17.1 us (14%)
  local copies, waits for them, and re-layouts  13.8 us (12%)
  waiting for transfers between devices  10.6 us (9%)
  matrix products  8.04 us (7%)
  other arithmetic  3.52 us (3%)
    pallas_call x1, Pallas kernels, token_stage(): pl.pallas_call(functools.partial(token_kernel, heads, rows_plane, planes,...  63.9 us
    ppermute x2, waiting for transfers between devices, shifted(): return lax.ppermute(block, axis, route)  8.09 us
    ppermute x1, starting transfers between devices, extended(): before = lax.ppermute(last, axis, up)  8 us
    ppermute x2, starting transfers between devices, shifted(): return lax.ppermute(block, axis, route)  7.21 us
    dot_general x5, matrix products, matmul(): result = jnp.dot(flat, weight, preferred_element_type=jnp.float32)  3.59 us
    div x1, local copies, waits for them, and re-layouts, on_device(): atom_mixed / jnp.transpose(atom_totals, (0, 1, 3, 2))[..., None]  3.3 us
    unnamed x27, local copies, waits for them, and re-layouts  2.88 us
    ppermute x1, waiting for transfers between devices, extended(): before = lax.ppermute(last, axis, up)  2.49 us
  transfers between devices with their start and end apart: 4, of which 3 were waited for; matrix products, arithmetic and copies ran while one was open for 3% of the time, Pallas kernels for 0%

profile of v1, /device:TPU:6, one launch (start us, length us, event | category | flops | bytes accessed | tf_op | source)
XLA Modules:
  0.0 117.9 jit_solution(8013374476516327260)
XLA Ops:
  0.6 1.3 %reshape.107.gain_ref = f32[1,768]{1,0:T(1,128)} reshape(f32[768]{0:T(1024)} %param.22) | data formatting | bytes 6144 | tf_op jit(solution)/shard_map/reshape | solution.py:566
  2.0 63.9 %shard_map.211 = (bf16[10,8,768]{2,1,0:T(8,128)(2,1)}, bf16[10,8,128]{2,1,0:T(8,128)(2,1)}) custom-call(bf16[10,8,768]{2,1,0:T(8,128)(2,1)} %x_ref.1, f32[1,768]{1,0:T(1,128)} %reshape.107.gain_ref, bf16[64,8,512]{2,1,0:T(8,128)(2,1)} %bias_hbm.1, bf16[768,768]{1,0:T(8,128)(2,1)} %wq_hbm.1, bf16[768,768]{1,0:T(8,128)(2,1)} %wk_hbm.1, ...), custom_call_target="tpu_custom_call" | custom-call | tf_op jit(solution)/shard_map/pallas_call | solution.py:520
  65.8 5.3 %collective-permute-start = (bf16[10,8,128]{2,1,0:T(8,128)(2,1)}, bf16[10,8,128]{2,1,0:T(8,128)(2,1)S(1)}, u32[]{:S(2)}, u32[]{:S(2)}) collective-permute-start(bf16[10,8,128]{2,1,0:T(8,128)(2,1)} %get-tuple-element.6), channel_id=1, source_target_pairs={{0,1},{1,2},{2,3},{3,4},{4,5},{5,6},{6,7},{7,8},{8,9},{9,10},{10,1... | collective-permute-start | bytes 61448 | tf_op jit(solution)/shard_map/ppermute | solution.py:24
  71.5 1.3 %collective-permute-done = bf16[10,8,128]{2,1,0:T(8,128)(2,1)S(1)} collective-permute-done((bf16[10,8,128]{2,1,0:T(8,128)(2,1)}, bf16[10,8,128]{2,1,0:T(8,128)(2,1)S(1)}, u32[]{:S(2)}, u32[]{:S(2)}) %collective-permute-start) | collective-permute-done | bytes 20512 | tf_op jit(solution)/shard_map/ppermute | solution.py:24
  72.8 1.0 fusion.42
  74.9 0.9 copy.55
  76.1 1.9 %collective-permute-start.2 = (bf16[10,48,256]{2,1,0:T(8,128)(2,1)S(1)}, bf16[10,48,256]{2,1,0:T(8,128)(2,1)S(1)}, u32[]{:S(2)}, u32[]{:S(2)}) collective-permute-start(bf16[10,48,256]{2,1,0:T(8,128)(2,1)S(1)} %copy.57), channel_id=1, source_target_pairs={{1,0},{2,1},{3,2},{4,3},{5,4},{6,5},{7,6},{8,7},{9,8},{10,9},{11,1... | collective-permute-start | bytes 737288 | tf_op jit(solution)/shard_map/ppermute | solution.py:35
  78.0 8.0 %collective-permute-start.1 = (bf16[10,48,256]{2,1,0:T(8,128)(2,1)}, bf16[10,48,256]{2,1,0:T(8,128)(2,1)S(1)}, u32[]{:S(2)}, u32[]{:S(2)}) collective-permute-start(bf16[10,48,256]{2,1,0:T(8,128)(2,1)} %copy.55), channel_id=1, source_target_pairs={{0,1},{1,2},{2,3},{3,4},{4,5},{5,6},{6,7},{7,8},{8,9},{9,10},{10,1... | collective-permute-start | bytes 737288 | tf_op jit(solution)/shard_map/ppermute | solution.py:34
  86.4 1.6 %reshape.109 = bf16[10,4,32,4,32]{4,3,2,1,0:T(4,128)(2,1)} reshape(bf16[10,128,128]{2,1,0:T(8,128)(2,1)S(1)} %convolution_convert_fusion.1) | data formatting | bytes 655360 | tf_op jit(solution)/shard_map/reshape | solution.py:635
  88.0 2.5 %collective-permute-done.1 = bf16[10,48,256]{2,1,0:T(8,128)(2,1)S(1)} collective-permute-done((bf16[10,48,256]{2,1,0:T(8,128)(2,1)}, bf16[10,48,256]{2,1,0:T(8,128)(2,1)S(1)}, u32[]{:S(2)}, u32[]{:S(2)}) %collective-permute-start.1) | collective-permute-done | bytes 245792 | tf_op jit(solution)/shard_map/ppermute | solution.py:34
  91.1 0.8 maximum_maximum_fusion
  92.0 0.7 slice_bitcast_fusion.1
  93.3 1.0 copy-done.1
  94.4 1.0 fusion.43
  95.4 1.6 %fusion = f32[10,4,4,32]{3,2,1,0:T(4,128)S(1)} fusion(f32[10,4,4,32,128]{4,3,2,1,0:T(8,128)S(1)} %get-tuple-element.29, f32[10,4,4,32]{3,2,1,0:T(4,128)S(1)} %get-tuple-element.28), kind=kLoop, calls=%fused_computation.4 | loop fusion | flops 1305600 | bytes 2662400 | tf_op jit(solution)/shard_map/reduce_sum | solution.py:654
  97.0 2.2 %bitcast_divide_fusion = f32[10,4,32,4,32]{2,4,3,1,0:T(8,128)} fusion(f32[10,4,4,32,128]{4,3,2,1,0:T(8,128)S(1)} %get-tuple-element.29, bf16[10,4,128,4,32]{2,4,3,0,1:T(8,128)(2,1)S(1)} %bitcast.52, f32[10,4,32,4]{2,3,1,0:T(4,128)S(1)} %bitcast.54, f32[10,4,4,32]{3,2,1,0:T(4,128)S(1)} %get-tuple-element.28), kind=kOutput, calls=%fused_computation.1 | convolution fusion | flops 43417600 | bytes 4628480 | tf_op jit(solution)/shard_map/swhqk,swkhd->swqhd/dot_general | solution.py:655
  99.2 3.3 %copy.64 = f32[10,4,32,4,32]{4,3,2,1,0:T(4,128)S(1)} copy(f32[10,4,32,4,32]{2,4,3,1,0:T(8,128)} %bitcast_divide_fusion) | data formatting | bytes 1310720 | tf_op jit(solution)/shard_map/div | solution.py:661
  102.6 1.9 %reshape.111 = f32[10,128,128]{2,1,0:T(8,128)} reshape(f32[10,4,32,4,32]{4,3,2,1,0:T(4,128)S(1)} %copy.64) | data formatting | bytes 1310720 | tf_op jit(solution)/shard_map/reshape | solution.py:662
  104.5 1.7 %fusion.8 = bf16[10,128,128]{1,2,0:T(8,128)(2,1)S(1)} fusion(f32[10,128,128]{1,2,0:T(8,128)S(1)} %get-tuple-element.27, f32[10,128,128]{2,1,0:T(8,128)} %reshape.111, bf16[128,128]{1,0:T(8,128)(2,1)S(1)} %copy-done.10, bf16[128,128]{1,0:T(8,128)(2,1)} %param.36, f32[128]{0:T(128)S(1)} %copy-done.8, f32[10,128]{1,0:T(8,128)S(1)} %add_rsqrt_fusion.1, ...), kind=kOutput, calls=%fused_computation.15 | convolution fusion | flops 86016000 | bytes 1714688 | tf_op jit(solution)/shard_map/dot_general | solution.py:49
  106.4 1.9 %collective-permute-start.3 = (bf16[10,8,128]{2,1,0:T(8,128)(2,1)S(1)}, bf16[10,8,128]{2,1,0:T(8,128)(2,1)S(1)}, u32[]{:S(2)}, u32[]{:S(2)}) collective-permute-start(bf16[10,8,128]{2,1,0:T(8,128)(2,1)S(1)} %slice.70), channel_id=1, source_target_pairs={{1,0},{2,1},{3,2},{4,3},{5,4},{6,5},{7,6},{8,7},{9,8},{10,9},{11,1... | collective-permute-start | bytes 61448 | tf_op jit(solution)/shard_map/ppermute | solution.py:24
  108.4 0.9 copy.68
  109.3 6.8 %collective-permute-done.3 = bf16[10,8,128]{2,1,0:T(8,128)(2,1)S(1)} collective-permute-done((bf16[10,8,128]{2,1,0:T(8,128)(2,1)S(1)}, bf16[10,8,128]{2,1,0:T(8,128)(2,1)S(1)}, u32[]{:S(2)}, u32[]{:S(2)}) %collective-permute-start.3) | collective-permute-done | bytes 20512 | tf_op jit(solution)/shard_map/ppermute | solution.py:24
  116.4 0.9 convolution_convert_fusion.4
  117.3 0.6 copy.92
  (47 shorter events, 3.6 us)
Async XLA Ops:
  0.6 115.7 %copy-start = (bf16[128,768]{1,0:T(8,128)(2,1)S(1)}, bf16[128,768]{1,0:T(8,128)(2,1)}, u32[]{:S(2)}) copy-start(bf16[128,768]{1,0:T(8,128)(2,1)} %param.39) | copy-start | bytes 589828
  2.0 69.3 %copy-start.3 = (bf16[4,32,512]{2,1,0:T(8,128)(2,1)S(1)}, bf16[4,32,512]{2,1,0:T(8,128)(2,1)}, u32[]{:S(2)}) copy-start(bf16[4,32,512]{2,1,0:T(8,128)(2,1)} %param.31) | copy-start | bytes 393220
  2.0 69.3 %copy-start.11 = (s32[128]{0:T(128)S(1)}, s32[128]{0:T(128)}, u32[]{:S(2)}) copy-start(s32[128]{0:T(128)} %param.30) | copy-start | bytes 1540
  2.0 69.3 %copy-start.2 = (bf16[10,128,128]{2,1,0:T(8,128)(2,1)S(1)}, bf16[10,128,128]{2,1,0:T(8,128)(2,1)}, u32[]{:S(2)}) copy-start(bf16[10,128,128]{2,1,0:T(8,128)(2,1)} %param.29) | copy-start | bytes 983044
  65.8 7.0 %collective-permute-start = (bf16[10,8,128]{2,1,0:T(8,128)(2,1)}, bf16[10,8,128]{2,1,0:T(8,128)(2,1)S(1)}, u32[]{:S(2)}, u32[]{:S(2)}) collective-permute-start(bf16[10,8,128]{2,1,0:T(8,128)(2,1)} %get-tuple-element.6), channel_id=1, source_target_pairs={{0,1},{1,2},{2,3},{3,4},{4,5},{5,6},{6,7},{7,8},{8,9},{9,10},{10,1... | collective-permute-start | bytes 61448 | tf_op jit(solution)/shard_map/ppermute | solution.py:24
  71.2 2.7 %copy-start.5 = (bf16[128,128]{1,0:T(8,128)(2,1)S(1)}, bf16[128,128]{1,0:T(8,128)(2,1)}, u32[]{:S(2)}) copy-start(bf16[128,128]{1,0:T(8,128)(2,1)} %param.35) | copy-start | bytes 98308
  71.2 2.7 %copy-start.8 = (f32[128]{0:T(128)S(1)}, f32[128]{0:T(128)}, u32[]{:S(2)}) copy-start(f32[128]{0:T(128)} %param.32) | copy-start | bytes 1540
  71.5 2.8 %copy-start.6 = (bf16[128,128]{1,0:T(8,128)(2,1)S(1)}, bf16[128,128]{1,0:T(8,128)(2,1)}, u32[]{:S(2)}) copy-start(bf16[128,128]{1,0:T(8,128)(2,1)} %param.34) | copy-start | bytes 98308
  74.9 11.1 %copy-start.7 = (bf16[128,128]{1,0:T(8,128)(2,1)S(1)}, bf16[128,128]{1,0:T(8,128)(2,1)}, u32[]{:S(2)}) copy-start(bf16[128,128]{1,0:T(8,128)(2,1)} %param.33) | copy-start | bytes 98308
  76.1 14.7 %collective-permute-start.2 = (bf16[10,48,256]{2,1,0:T(8,128)(2,1)S(1)}, bf16[10,48,256]{2,1,0:T(8,128)(2,1)S(1)}, u32[]{:S(2)}, u32[]{:S(2)}) collective-permute-start(bf16[10,48,256]{2,1,0:T(8,128)(2,1)S(1)} %copy.57), channel_id=1, source_target_pairs={{1,0},{2,1},{3,2},{4,3},{5,4},{6,5},{7,6},{8,7},{9,8},{10,9},{11,1... | collective-permute-start | bytes 737288 | tf_op jit(solution)/shard_map/ppermute | solution.py:35
  78.0 12.5 %collective-permute-start.1 = (bf16[10,48,256]{2,1,0:T(8,128)(2,1)}, bf16[10,48,256]{2,1,0:T(8,128)(2,1)S(1)}, u32[]{:S(2)}, u32[]{:S(2)}) collective-permute-start(bf16[10,48,256]{2,1,0:T(8,128)(2,1)} %copy.55), channel_id=1, source_target_pairs={{0,1},{1,2},{2,3},{3,4},{4,5},{5,6},{6,7},{7,8},{8,9},{9,10},{10,1... | collective-permute-start | bytes 737288 | tf_op jit(solution)/shard_map/ppermute | solution.py:34
  93.0 1.3 %copy-start.1 = (bf16[10,4,32,4,32]{4,3,2,1,0:T(4,128)(2,1)S(1)}, bf16[10,4,32,4,32]{4,3,2,1,0:T(4,128)(2,1)}, u32[]{:S(2)}) copy-start(bf16[10,4,32,4,32]{4,3,2,1,0:T(4,128)(2,1)} %reshape.109) | copy-start | bytes 983044
  102.5 1.9 %copy-start.10 = (bf16[128,128]{1,0:T(8,128)(2,1)S(1)}, bf16[128,128]{1,0:T(8,128)(2,1)}, u32[]{:S(2)}) copy-start(bf16[128,128]{1,0:T(8,128)(2,1)} %param.37) | copy-start | bytes 98308
  104.5 11.9 %copy-start.9 = (f32[128]{0:T(128)S(1)}, f32[128]{0:T(128)}, u32[]{:S(2)}) copy-start(f32[128]{0:T(128)} %param.38) | copy-start | bytes 1540
  106.2 11.1 %copy-start.4 = (bf16[10,8,768]{2,1,0:T(8,128)(2,1)S(1)}, bf16[10,8,768]{2,1,0:T(8,128)(2,1)}, u32[]{:S(2)}) copy-start(bf16[10,8,768]{2,1,0:T(8,128)(2,1)} %get-tuple-element.35) | copy-start | bytes 368644
  106.4 9.7 %collective-permute-start.3 = (bf16[10,8,128]{2,1,0:T(8,128)(2,1)S(1)}, bf16[10,8,128]{2,1,0:T(8,128)(2,1)S(1)}, u32[]{:S(2)}, u32[]{:S(2)}) collective-permute-start(bf16[10,8,128]{2,1,0:T(8,128)(2,1)S(1)} %slice.70), channel_id=1, source_target_pairs={{1,0},{2,1},{3,2},{4,3},{5,4},{6,5},{7,6},{8,7},{9,8},{10,9},{11,1... | collective-permute-start | bytes 61448 | tf_op jit(solution)/shard_map/ppermute | solution.py:24

commit v2 on v1

--- a/solution.py
+++ b/solution.py
@@ -10,44 +10,9 @@
 
 MESH = pl.DeviceIdType.MESH
 LANES = 128
-
 WQ = 32
 WK = 128
-
-
 EPSILON = 1e-05
-
-
-def shifted(block, axis, distance):
-    devices = range(lax.axis_size(axis))
-    route = [(i - distance, i) for i in devices if i - distance in devices]
-    return lax.ppermute(block, axis, route)
-
-
-def extended(array, sides, width):
-    for axis, dim in sides:
-        count, length = (lax.axis_size(axis), array.shape[dim])
-        up = [(i, (i + 1) % count) for i in range(count - 1)]
-        down = [(j, i) for i, j in up]
-        last = lax.slice_in_dim(array, length - width, length, axis=dim)
-        initial = lax.slice_in_dim(array, 0, width, axis=dim)
-        before = lax.ppermute(last, axis, up)
-        after = lax.ppermute(initial, axis, down)
-        array = jnp.concatenate([before, array, after], axis=dim)
-    return array
-
-
-def layer_norm(inputs, gain):
-    values = inputs.astype(jnp.float32)
-    center = values - jnp.mean(values, axis=-1, keepdims=True)
-    spread = jnp.mean(center * center, axis=-1, keepdims=True)
-    return center * lax.rsqrt(spread + EPSILON) * gain
-
-
-def matmul(inputs, weight):
-    flat = inputs.reshape(-1, inputs.shape[-1])
-    result = jnp.dot(flat, weight, preferred_element_type=jnp.float32)
-    return result.reshape(inputs.shape[:-1] + (weight.shape[1],))
 
 
 def lane_index(shape):
@@ -69,7 +34,7 @@
     return roll_left(values[:, tile * LANES : (tile + 2) * LANES], rest)[:, :LANES]
 
 
-def token_kernel(
+def pass_kernel(
     heads,
     rows_plane,
     planes,
@@ -83,8 +48,20 @@
     wg_hbm,
     wo_hbm,
     wc_hbm,
+    atom_hbm,
+    token_ref,
+    abias_hbm,
+    again_ref,
+    aq_hbm,
+    ak_hbm,
+    av_hbm,
+    ag_hbm,
+    ao_hbm,
+    pgain_ref,
+    wp_hbm,
     update_ref,
-    cond_ref,
+    result_ref,
+    pool_ref,
     bias_in,
     wq,
     wk,
@@ -111,11 +88,29 @@
     ob_send,
     ob_recv,
     gate_s,
+    atoms,
+    token_rim,
+    abias_in,
+    abias,
+    w_kv,
+    w_qg,
+    w_ao,
+    wp,
+    selector,
+    cond_rim,
+    state_s,
+    kv_s,
+    qg_s,
+    gated_s,
+    pool_send,
+    pool_recv,
     load_sem,
     a2a_send_sem,
     a2a_recv_sem,
     ring_send_sem,
     ring_recv_sem,
+    near_send_sem,
+    near_recv_sem,
 ):
     samples, tokens, width = x_ref.shape
     head_dim = width // heads
@@ -138,6 +133,29 @@
 
     def head_of(p):
         return (p // n_col) // 2 * n_col + p % n_col, (p // n_col) % 2
+
+    devices = lax.axis_size("row") * n_col
+    device = row * n_col + col
+    atom_dev, atom_width = result_ref.shape[1:]
+    reach = (WK - WQ) // 2
+    ext = atom_dev + 2 * reach
+    windows = atom_dev // WQ
+    atom_heads = abias_hbm.shape[2] // WK
+    atom_hdim = atom_width // atom_heads
+
+    def near(step):
+        other = lax.rem(device + step + devices, devices)
+        return (other // n_col, other % n_col)
+
+    def near_copy(source, target, step, which):
+        return pltpu.make_async_remote_copy(
+            src_ref=source,
+            dst_ref=target,
+            send_sem=near_send_sem.at[which],
+            recv_sem=near_recv_sem.at[which],
+            device_id=near(step),
+            device_id_type=MESH,
+        )
 
     def ring_device(step):
         other = lax.rem(z + step + planes, planes)
@@ -154,6 +172,14 @@
                 (wg_hbm, wg),
                 (wo_hbm, wo),
                 (wc_hbm, wc),
+                (atom_hbm, atoms.at[:, pl.ds(reach, atom_dev)]),
+                (abias_hbm, abias_in),
+                (ak_hbm, w_kv.at[:, pl.ds(0, atom_width)]),
+                (av_hbm, w_kv.at[:, pl.ds(atom_width, atom_width)]),
+                (aq_hbm, w_qg.at[:, pl.ds(0, atom_width)]),
+                (ag_hbm, w_qg.at[:, pl.ds(atom_width, atom_width)]),
+                (ao_hbm, w_ao),
+                (wp_hbm, wp),
             )
         )
     ]
@@ -171,6 +197,8 @@
     lax.fori_loop(1, peers, greet, 0)
     for step in (1, -1):
         pl.semaphore_signal(barrier, inc=1, device_id=ring_device(step), device_id_type=MESH)
+    for step in (1, -1, 2, -2):
+        pl.semaphore_signal(barrier, inc=1, device_id=near(step), device_id_type=MESH)
 
     loads[0].wait()
     columns = bias_in.shape[2]
@@ -212,7 +240,7 @@
     piece = planes * 2 * tokens
     bias_send[...] = bias_t[...].astype(jnp.bfloat16).reshape(heads, piece, LANES)
 
-    pl.semaphore_wait(barrier, peers + 1)
+    pl.semaphore_wait(barrier, peers + 5)
 
     def send_bias(i, carry):
         p = lax.rem(me + i, peers)
@@ -296,6 +324,19 @@
 
     lax.fori_loop(1, peers, send_q, 0)
     q_recv[me] = q_send[my_core, my_head]
+
+    near_sends = [
+        near_copy(
+            atom_hbm.at[:, pl.ds(atom_dev - reach, reach)], atoms.at[:, pl.ds(0, reach)], 1, 0
+        ),
+        near_copy(
+            atom_hbm.at[:, pl.ds(0, reach)], atoms.at[:, pl.ds(reach + atom_dev, reach)], -1, 1
+        ),
+        near_copy(token_ref, token_rim.at[0], 1, 2),
+        near_copy(token_ref, token_rim.at[1], -1, 3),
+    ]
+    for copy in near_sends:
+        copy.start()
 
     loads[4].wait()
     gate_s[...] = jnp.dot(normed, wg[...], preferred_element_type=jnp.float32).astype(jnp.bfloat16)
@@ -381,6 +422,35 @@
                 .astype(jnp.bfloat16)
             )
 
+    def atom_setup():
+        for load in loads[7:]:
+            load.wait()
+        for copy in near_sends:
+            copy.wait_recv()
+        base = (device - 2) * tokens
+        ids = lax.broadcasted_iota(jnp.int32, (atom_dev, atom_dev), 0)
+        eye_a = (ids == lane_index((atom_dev, atom_dev))).astype(jnp.bfloat16)
+        chosen = []
+        for own, first_atom, count in (
+            (token_rim[0], atom_dev - reach, reach),
+            (token_ref[...], 0, atom_dev),
+            (token_rim[1], 0, reach),
+        ):
+            hit = ((own - base) == ids).astype(jnp.bfloat16)
+            across = lax.dot_general(
+                eye_a, hit, (((1,), (1,)), ((), ())), preferred_element_type=jnp.float32
+            )
+            chosen.append(across[first_atom : first_atom + count])
+        selector[...] = jnp.concatenate(chosen, axis=0).astype(jnp.bfloat16)
+        for w in range(windows):
+            place = device * atom_dev + w * WQ - reach + lane_index((WQ, WK))
+            valid = (place >= 0) & (place < devices * atom_dev)
+            rows = abias_in[w].astype(jnp.float32)
+            for h in range(atom_heads):
+                abias[w, h * WQ : (h + 1) * WQ, :] = jnp.where(
+                    valid, rows[:, h * WK : (h + 1) * WK] * log2e, -1e9
+                )
+
     def attend(s):
         q_one = q_all[s][:, :head_dim]
         peak = None
@@ -437,6 +507,7 @@
         @pl.when(k == half_ring - 1)
         def _():
             bias_stage()
+            atom_setup()
 
         @pl.when(k >= half_ring)
         def _():
@@ -484,8 +555,99 @@
     update_ref[...] = update.reshape(samples, tokens, width).astype(jnp.bfloat16)
     loads[6].wait()
     cond = jnp.dot(update.astype(jnp.bfloat16), wc[...], preferred_element_type=jnp.float32)
-    cond_ref[...] = cond.reshape(samples, tokens, cond.shape[-1]).astype(jnp.bfloat16)
-
+    cond_rim[2] = cond.astype(jnp.bfloat16)
+    cond_sends = [
+        near_copy(cond_rim.at[2], cond_rim.at[1], 1, 4),
+        near_copy(cond_rim.at[2], cond_rim.at[0], 2, 5),
+        near_copy(cond_rim.at[2], cond_rim.at[3], -1, 6),
+    ]
+    for copy in cond_sends:
+        copy.start()
+    update_ref[...] = update.reshape(samples, tokens, width).astype(jnp.bfloat16)
+    for copy in cond_sends:
+        copy.wait_recv()
+
+    def norm(rows, gain):
+        middle = rows - jnp.mean(rows, axis=-1, keepdims=True)
+        spread = jnp.mean(middle * middle, axis=-1, keepdims=True)
+        return middle * lax.rsqrt(spread + EPSILON) * gain
+
+    conds = [
+        cond_rim[b].astype(jnp.float32).reshape(samples, tokens, atom_width) for b in range(4)
+    ]
+    chooser = selector[:, : 4 * tokens]
+    atom_gain = again_ref[...]
+    for s in range(samples):
+        near_cond = jnp.concatenate([conds[b][s] for b in range(4)], axis=0).astype(jnp.bfloat16)
+        carried = jnp.dot(chooser, near_cond, preferred_element_type=jnp.float32)
+        state = atoms[s].astype(jnp.float32) + carried
+        own_state = state[reach : reach + atom_dev]
+        state_s[s] = own_state
+        atom_normed = norm(state, atom_gain).astype(jnp.bfloat16)
+        kv_s[s] = jnp.dot(atom_normed, w_kv[...], preferred_element_type=jnp.float32).astype(
+            jnp.bfloat16
+        )
+        qg_s[s] = jnp.dot(
+            atom_normed[reach : reach + atom_dev], w_qg[...], preferred_element_type=jnp.float32
+        ).astype(jnp.bfloat16)
+
+    atom_factor = log2e / math.sqrt(atom_hdim)
+    head_lane = lane_index((WQ, atom_width)) // atom_hdim
+    ones_key = jnp.ones((WK, LANES), jnp.bfloat16)
+
+    def atom_attend(s, carry):
+        for w in range(windows):
+            q_rows = qg_s[s, w * WQ : (w + 1) * WQ, :atom_width].astype(jnp.float32)
+            spread_q = jnp.concatenate(
+                [jnp.where(head_lane == h, q_rows, 0.0) for h in range(atom_heads)], axis=0
+            ).astype(jnp.bfloat16)
+            k_rows = kv_s[s, w * WQ : w * WQ + WK, :atom_width]
+            v_rows = kv_s[s, w * WQ : w * WQ + WK, atom_width:]
+            raw = lax.dot_general(
+                spread_q, k_rows, (((1,), (1,)), ((), ())), preferred_element_type=jnp.float32
+            )
+            score = raw * atom_factor + abias[w]
+            weights = jnp.exp2(score - jnp.max(score, axis=-1, keepdims=True))
+            mixed = jnp.dot(
+                weights.astype(jnp.bfloat16),
+                jnp.concatenate([v_rows, ones_key], axis=1),
+                preferred_element_type=jnp.float32,
+            )
+            share = mixed[:, :atom_width] / mixed[:, atom_width:]
+            joined = share[:WQ]
+            for h in range(1, atom_heads):
+                joined = jnp.where(head_lane == h, share[h * WQ : (h + 1) * WQ], joined)
+            gate = qg_s[s, w * WQ : (w + 1) * WQ, atom_width:].astype(jnp.float32)
+            gated_s[s, w * WQ : (w + 1) * WQ, :] = (joined * jax.nn.sigmoid(gate)).astype(
+                jnp.bfloat16
+            )
+        return carry
+
+    lax.fori_loop(0, samples, atom_attend, 0)
+
+    local = token_ref[...] - (device - 1) * tokens
+    gather = (local == lax.broadcasted_iota(jnp.int32, (2 * tokens, atom_dev), 0)).astype(
+        jnp.bfloat16
+    )
+    sums = []
+    for s in range(samples):
+        result = (
+            state_s[s] + jnp.dot(gated_s[s], w_ao[...], preferred_element_type=jnp.float32)
+        ).astype(jnp.bfloat16)
+        result_ref[s] = result
+        sums.append(jnp.dot(gather, result, preferred_element_type=jnp.float32))
+    pool_send[...] = jnp.concatenate([one[:tokens] for one in sums], axis=0).astype(jnp.bfloat16)
+    pool_copy = near_copy(pool_send, pool_recv, -1, 7)
+    pool_copy.start()
+    pool_copy.wait_recv()
+    arrived = jnp.where(device < devices - 1, pool_recv[...].astype(jnp.float32), 0.0)
+    own_sums = jnp.concatenate([one[tokens:] for one in sums], axis=0) + arrived
+    pooled = norm(own_sums, pgain_ref[...]).astype(jnp.bfloat16)
+    token_pool = jnp.dot(pooled, wp[...], preferred_element_type=jnp.float32)
+    pool_ref[...] = token_pool.reshape(samples, tokens, width).astype(jnp.bfloat16)
+
+    for copy in near_sends + cond_sends + [pool_copy]:
+        copy.wait_send()
     for which, buffer in ((0, bias_recv), (1, kv_recv), (2, q_recv), (3, oa_recv), (4, ob_recv)):
         wait_all(buffer, a2a_send_sem.at[which])
 
@@ -498,8 +660,10 @@
     lax.fori_loop(0, per_core, drain, 0)
 
 
-def token_stage(
-    single, pair_bias, token_gain, w_query, w_key, w_value, w_gate, w_out, w_cond, n_row, n_col
+def diffusion_pass(
+    single, pair_bias, token_gain, w_query, w_key, w_value, w_gate, w_out, w_cond, atom_single,
+    atom_token, atom_bias, atom_gain, atom_query, atom_key, atom_value, atom_gate, atom_out,
+    pool_gain, w_pool, n_row, n_col
 ):
     samples, tokens, width = single.shape
     queries, _, columns = pair_bias.shape
@@ -512,19 +676,28 @@
     plane_tokens = peers * tokens
     padded = -(-per_core * tokens // 16) * 16
     piece = planes * 2 * tokens
-    cond_width = w_cond.shape[1]
+    _, atom_dev, atom_width = atom_single.shape
+    reach = (WK - WQ) // 2
+    ext = atom_dev + 2 * reach
+    windows = atom_dev // WQ
+    atom_heads = atom_bias.shape[2] // WK
     early = (per_core - 1) * tokens
     bf16, f32 = jnp.bfloat16, jnp.float32
     vmem = pl.BlockSpec(memory_space=pltpu.VMEM)
     anywhere = pl.BlockSpec(memory_space=pl.ANY)
     return pl.pallas_call(
-        functools.partial(token_kernel, heads, rows_plane, planes, n_col),
+        functools.partial(pass_kernel, heads, rows_plane, planes, n_col),
         out_shape=(
             jax.ShapeDtypeStruct((samples, tokens, width), bf16),
-            jax.ShapeDtypeStruct((samples, tokens, cond_width), bf16),
+            jax.ShapeDtypeStruct(atom_single.shape, bf16),
+            jax.ShapeDtypeStruct((samples, tokens, width), bf16),
         ),
-        in_specs=[vmem, vmem] + [anywhere] * 7,
-        out_specs=(vmem, vmem),
+        in_specs=[vmem, vmem]
+        + [anywhere] * 8
+        + [vmem, anywhere, vmem]
+        + [anywhere] * 5
+        + [vmem, anywhere],
+        out_specs=(vmem, vmem, vmem),
         scratch_shapes=[
             pltpu.VMEM(pair_bias.shape, bf16),
             pltpu.VMEM(w_query.shape, bf16),
@@ -552,11 +725,29 @@
             pltpu.VMEM((peers, 2 * tokens, LANES), bf16),
             pltpu.VMEM((peers, 2 * tokens, LANES), bf16),
             pltpu.VMEM((samples * tokens, width), bf16),
-            pltpu.SemaphoreType.DMA((7,)),
+            pltpu.VMEM((samples, ext, atom_width), bf16),
+            pltpu.VMEM((2, 1, atom_dev), jnp.int32),
+            pltpu.VMEM(atom_bias.shape, bf16),
+            pltpu.VMEM((windows, atom_heads * WQ, WK), f32),
+            pltpu.VMEM((atom_width, 2 * atom_width), bf16),
+            pltpu.VMEM((atom_width, 2 * atom_width), bf16),
+            pltpu.VMEM(atom_out.shape, bf16),
+            pltpu.VMEM(w_pool.shape, bf16),
+            pltpu.VMEM((ext, atom_dev), bf16),
+            pltpu.VMEM((4, samples * tokens, atom_width), bf16),
+            pltpu.VMEM((samples, atom_dev, atom_width), f32),
+            pltpu.VMEM((samples, ext, 2 * atom_width), bf16),
+            pltpu.VMEM((samples, atom_dev, 2 * atom_width), bf16),
+            pltpu.VMEM((samples, atom_dev, atom_width), bf16),
+            pltpu.VMEM((samples * tokens, atom_width), bf16),
+            pltpu.VMEM((samples * tokens, atom_width), bf16),
+            pltpu.SemaphoreType.DMA((15,)),
             pltpu.SemaphoreType.DMA((5,)),
             pltpu.SemaphoreType.DMA((5,)),
             pltpu.SemaphoreType.DMA((2, planes // 2, per_core)),
             pltpu.SemaphoreType.DMA((2, planes // 2, per_core)),
+            pltpu.SemaphoreType.DMA((8,)),
+            pltpu.SemaphoreType.DMA((8,)),
         ],
         compiler_params=pltpu.CompilerParams(
             collective_id=1, has_side_effects=True, vmem_limit_bytes=56 * 1024 * 1024
@@ -571,110 +762,26 @@
         w_gate,
         w_out,
         w_cond,
+        atom_single,
+        atom_token.reshape(1, atom_dev),
+        atom_bias,
+        atom_gain.reshape(1, atom_width),
+        atom_query,
+        atom_key,
+        atom_value,
+        atom_gate,
+        atom_out,
+        pool_gain.reshape(1, atom_width),
+        w_pool,
     )
 
 
-def on_device(
-    single,
-    pair_bias,
-    token_gain,
-    w_query,
-    w_key,
-    w_value,
-    w_gate,
-    w_out,
-    w_cond,
-    atom_single,
-    atom_token,
-    atom_bias,
-    atom_gain,
-    atom_query,
-    atom_key,
-    atom_value,
-    atom_gate,
-    atom_out,
-    pool_gain,
-    w_pool,
-):
-    n_row = lax.axis_size("row")
-    n_col = lax.axis_size("col")
-    samples, tok_dev, width = single.shape
-    token_update, cond = token_stage(
-        single, pair_bias, token_gain, w_query, w_key, w_value, w_gate, w_out, w_cond, n_row, n_col
-    )
-    cond_lower = shifted(cond, ("row", "col"), 1)
-    cond_rim = jnp.concatenate([cond_lower, cond], axis=1)
-    device = lax.axis_index(("row", "col"))
-    atom_dev = atom_single.shape[1]
-    atom_width = atom_single.shape[2]
-    local_token = atom_token - (device - 1) * tok_dev
-    selector = (local_token[:, None] == jnp.arange(2 * tok_dev, dtype=jnp.int32)[None, :]).astype(
-        jnp.bfloat16
-    )
-    carried = jnp.einsum("at,stc->sac", selector, cond_rim, preferred_element_type=jnp.float32)
-    atom_state = atom_single.astype(jnp.float32) + carried
-    atom_normed = layer_norm(atom_state, atom_gain).astype(jnp.bfloat16)
-    atom_q = matmul(atom_normed, atom_query).astype(jnp.bfloat16)
-    atom_k = matmul(atom_normed, atom_key).astype(jnp.bfloat16)
-    atom_v = matmul(atom_normed, atom_value).astype(jnp.bfloat16)
-    atom_g = matmul(atom_normed, atom_gate).astype(jnp.bfloat16)
-    reach = (WK - WQ) // 2
-    kv_rim = extended(jnp.concatenate([atom_k, atom_v], axis=-1), ((("row", "col"), 1),), reach)
-    windows = atom_dev // WQ
-    kv_window = jnp.stack(
-        [
-            lax.slice_in_dim(kv_rim, window * WQ, window * WQ + WK, axis=1)
-            for window in range(windows)
-        ],
-        axis=1,
-    )
-    atom_heads = atom_bias.shape[2] // WK
-    atom_hdim = atom_width // atom_heads
-    key_window = kv_window[..., :atom_width].reshape(samples, windows, WK, atom_heads, atom_hdim)
-    value_window = kv_window[..., atom_width:].reshape(samples, windows, WK, atom_heads, atom_hdim)
-    query_window = atom_q.reshape(samples, windows, WQ, atom_heads, atom_hdim)
-    total_atoms = atom_dev * n_row * n_col
-    position = (
-        device * atom_dev
-        + jnp.arange(windows, dtype=jnp.int32)[:, None] * WQ
-        + jnp.arange(WK, dtype=jnp.int32)[None, :]
-        - reach
-    )
-    valid = (position >= 0) & (position < total_atoms)
-    window_bias = jnp.transpose(
-        atom_bias.reshape(windows, WQ, atom_heads, WK), (0, 2, 1, 3)
-    ).astype(jnp.float32)
-    atom_scores = jnp.einsum(
-        "swqhd,swkhd->swhqk", query_window, key_window, preferred_element_type=jnp.float32
-    )
-    atom_scores = atom_scores * (1.0 / math.sqrt(atom_hdim)) + window_bias[None]
-    atom_scores = jnp.where(valid[None, :, None, None, :], atom_scores, -1000000000.0)
-    atom_maxima = jnp.max(atom_scores, axis=-1, keepdims=True)
-    atom_weights = jnp.exp(atom_scores - atom_maxima)
-    atom_totals = jnp.sum(atom_weights, axis=-1)
-    atom_mixed = jnp.einsum(
-        "swhqk,swkhd->swqhd",
-        atom_weights.astype(jnp.bfloat16),
-        value_window,
-        preferred_element_type=jnp.float32,
-    )
-    atom_mixed = atom_mixed / jnp.transpose(atom_totals, (0, 1, 3, 2))[..., None]
-    atom_mixed = atom_mixed.reshape(samples, atom_dev, atom_width)
-    atom_gated = (atom_mixed * jax.nn.sigmoid(atom_g.astype(jnp.float32))).astype(jnp.bfloat16)
-    atom_result = (atom_state + matmul(atom_gated, atom_out)).astype(jnp.bfloat16)
-    sums_local = jnp.einsum(
-        "at,sac->stc", selector, atom_result, preferred_element_type=jnp.float32
-    )
-    from_next = shifted(sums_local[:, :tok_dev].astype(jnp.bfloat16), ("row", "col"), -1).astype(
-        jnp.float32
-    )
-    own_sums = sums_local[:, tok_dev:] + from_next
-    pooled = layer_norm(own_sums, pool_gain).astype(jnp.bfloat16)
-    token_pool = matmul(pooled, w_pool).astype(jnp.bfloat16)
-    return (token_update, atom_result, token_pool)
-
-
 def solution(mesh):
+    n_row, n_col = mesh.shape["row"], mesh.shape["col"]
+
+    def on_device(*arrays):
+        return diffusion_pass(*arrays, n_row, n_col)
+
     placed = (
         P(None, ("row", "col"), None),
         P("row", "col", None),

time: 120 us -> 99.5 us (0.83); the launches traced: 118 us -> 99.3 us
  Pallas kernels: 63.9 us -> 92.5 us
  starting transfers between devices: 17.1 us -> 0 us
  waiting for transfers between devices: 10.6 us -> 0 us
  matrix products: 8.04 us -> 0 us
  local copies, waits for them, and re-layouts: 13.8 us -> 6.1 us
  other arithmetic: 3.52 us -> 0 us
    pallas_call x1, Pallas kernels: 63.9 us -> 92.5 us  [diffusion_pass(): pl.pallas_call(functools.partial(pass_kernel, heads, rows_plane, planes,...]
    ppermute x4 -> x0, starting transfers between devices: 17.1 us -> none  [the longest x1 8 us: extended(): before = lax.ppermute(last, axis, up)]
    ppermute x4 -> x0, waiting for transfers between devices: 10.6 us -> none  [the longest x2 8.09 us: shifted(): return lax.ppermute(block, axis, route)]
    dot_general x9 -> x0, matrix products: 8.04 us -> none  [the longest x5 3.59 us: matmul(): result = jnp.dot(flat, weight, preferred_element_type=jnp.float32)]
    reshape x3 -> x1, local copies, waits for them, and re-layouts: 4.83 us -> 1.27 us  [diffusion_pass(): token_gain.reshape(1, width)]
    div x1 -> x0, local copies, waits for them, and re-layouts: 3.3 us -> none  [on_device(): atom_mixed / jnp.transpose(atom_totals, (0, 1, 3, 2))[..., None]]
    reduce_sum x4 -> x0, other arithmetic: 1.97 us -> none  [the longest x1 1.65 us: on_device(): atom_totals = jnp.sum(atom_weights, axis=-1)]
    unnamed x27 -> x3, local copies, waits for them, and re-layouts: 2.88 us -> 4.84 us
  transfers between devices with their start and end apart: 4 -> 0, of which waited for: 3 -> 0; matrix products, arithmetic and copies ran while one was open for 3% -> 0% of each run, Pallas kernels for 0% -> 0%
where the time goes in v2:
time: 99.5 us; the launch traced here: 99.3 us
  Pallas kernels  92.5 us (93%)
  local copies, waits for them, and re-layouts  6.1 us (6%)
    pallas_call x1, Pallas kernels, diffusion_pass(): pl.pallas_call(functools.partial(pass_kernel, heads, rows_plane, planes,...  92.5 us
    unnamed x3, local copies, waits for them, and re-layouts  4.84 us

profile of v2, /device:TPU:6, one launch (start us, length us, event | category | flops | bytes accessed | tf_op | source)
XLA Modules:
  0.0 99.3 jit_solution(18430782374954242793)
XLA Ops:
  0.6 1.3 %reshape.18.gain_ref = f32[1,768]{1,0:T(1,128)} reshape(f32[768]{0:T(1024)} %param.22) | data formatting | bytes 6144 | tf_op jit(solution)/shard_map/reshape | solution.py:757
  1.9 92.5 %shard_map.211 = (bf16[10,8,768]{2,1,0:T(8,128)(2,1)}, bf16[10,128,128]{2,1,0:T(8,128)(2,1)}, bf16[10,8,768]{2,1,0:T(8,128)(2,1)}) custom-call(bf16[10,8,768]{2,1,0:T(8,128)(2,1)} %x_ref.1, f32[1,768]{1,0:T(1,128)} %reshape.18.gain_ref, bf16[64,8,512]{2,1,0:T(8,128)(2,1)} %bias_hbm.1, bf16[768,768]{1,0:T(8,128)(2,1)} %wq_hbm.1, bf16[768,768]{1,0:T(8,128)(2,1)} %wk_hbm.1, ...), custom_call_target="tpu_custom_call" | custom-call | tf_op jit(solution)/shard_map/pallas_call | solution.py:688
  94.4 1.6 %copy.26 = bf16[10,8,768]{2,1,0:T(8,128)(2,1)} copy(bf16[10,8,768]{2,1,0:T(8,128)(2,1)} %get-tuple-element.6) | data formatting | bytes 245760
  96.0 1.7 %copy.27 = bf16[10,128,128]{2,1,0:T(8,128)(2,1)} copy(bf16[10,128,128]{2,1,0:T(8,128)(2,1)} %get-tuple-element.7) | data formatting | bytes 655360
  97.7 1.6 %copy.28 = bf16[10,8,768]{2,1,0:T(8,128)(2,1)} copy(bf16[10,8,768]{2,1,0:T(8,128)(2,1)} %get-tuple-element.8) | data formatting | bytes 245760

commit v3 on v2

v3 whole, which is shorter than its diff:
```python
import functools
import math

import jax
import jax.numpy as jnp
from jax import lax
from jax.experimental import pallas as pl
from jax.experimental.pallas import tpu as pltpu
from jax.sharding import PartitionSpec as P

MESH = pl.DeviceIdType.MESH
LANES = 128
WQ = 32
WK = 128
EPSILON = 1e-05


def lane_index(shape):
    return lax.broadcasted_iota(jnp.int32, shape, len(shape) - 1)


def rolled(values, amount):
    amount = amount % LANES
    return pltpu.roll(values, amount, values.ndim - 1) if amount else values


def placed_at(values, start, count, target):
    tile, rest = divmod(start, LANES)
    first = rolled(values[:, tile * LANES : (tile + 1) * LANES], target - rest)
    if rest + count <= LANES:
        return first
    second = rolled(values[:, (tile + 1) * LANES : (tile + 2) * LANES], target - rest)
    return jnp.where(lane_index(first.shape) < target + LANES - rest, first, second)


def norm(rows, gain):
    center = rows - jnp.mean(rows, axis=-1, keepdims=True)
    spread = jnp.mean(center * center, axis=-1, keepdims=True)
    return center * lax.rsqrt(spread + EPSILON) * gain


def pass_kernel(
    heads,
    rows_plane,
    planes,
    n_col,
    x_ref,
    gain_ref,
    bias_hbm,
    wq_hbm,
    wk_hbm,
    wv_hbm,
    wg_hbm,
    wo_hbm,
    wc_hbm,
    atom_hbm,
    token_ref,
    abias_hbm,
    again_ref,
    aq_hbm,
    ak_hbm,
    av_hbm,
    ag_hbm,
    ao_hbm,
    update_ref,
    result_ref,
    sums_ref,
    bias_in,
    wq,
    wk,
    wv,
    wg,
    wo,
    wc,
    bias_f,
    bias_t,
    bias_send,
    bias_recv,
    bias_keys,
    bias_all,
    qkv_send,
    qkv_recv,
    kv_ring,
    scores,
    out_f,
    out_send,
    out_recv,
    gate_s,
    w_oc,
    atoms,
    token_rim,
    abias_in,
    abias,
    w_kv,
    w_qg,
    w_ao,
    selector,
    cond_rim,
    state_s,
    kv_s,
    qg_s,
    gated_s,
    pool_send,
    pool_recv,
    load_sem,
    a2a_send_sem,
    a2a_recv_sem,
    ring_send_sem,
    ring_recv_sem,
    near_send_sem,
    near_recv_sem,
):
    samples, tokens, width = x_ref.shape
    head_dim = width // heads
    per_core = samples // 2
    half_ring = planes // 2
    peers = rows_plane * n_col
    flat = samples * tokens
    part = per_core * tokens
    queries = tokens * n_col
    plane_tokens = peers * tokens

    row, col = lax.axis_index("row"), lax.axis_index("col")
    z, r4 = row // rows_plane, row % rows_plane
    me = r4 * n_col + col
    my_core = r4 % 2
    my_head = (r4 // 2) * n_col + col

    my_ylo = r4 // 2
    others = [
        (dy, dcore, dc)
        for dc in range(n_col)
        for dy in range(2)
        for dcore in range(2)
        if dy or dcore or dc
    ]

    def wrapped(value, size):
        return jnp.where(value >= size, value - size, value)

    def peer(dy, dcore, dc):
        return wrapped(my_ylo + dy, 2), wrapped(my_core + dcore, 2), wrapped(col + dc, n_col)

    def device_of(ylo, core, c):
        return (z * rows_plane + ylo * 2 + core, c)

    devices = lax.axis_size("row") * n_col
    device = row * n_col + col
    atom_dev, atom_width = result_ref.shape[1:]
    reach = (WK - WQ) // 2
    ext = atom_dev + 2 * reach
    windows = atom_dev // WQ
    atom_heads = abias_hbm.shape[2] // WK
    atom_hdim = atom_width // atom_heads

    def near(step):
        other = lax.rem(device + step + devices, devices)
        return (other // n_col, other % n_col)

    def near_copy(source, target, step, which):
        return pltpu.make_async_remote_copy(
            src_ref=source,
            dst_ref=target,
            send_sem=near_send_sem.at[which],
            recv_sem=near_recv_sem.at[which],
            device_id=near(step),
            device_id_type=MESH,
        )

    def ring_device(step):
        other = lax.rem(z + step + planes, planes)
        return (other * rows_plane + r4, col)

    loads = [
        pltpu.make_async_copy(source, target, load_sem.at[i])
        for i, (source, target) in enumerate(
            (
                (wk_hbm, wk),
                (wv_hbm, wv),
                (wq_hbm, wq),
                (bias_hbm, bias_in),
                (wg_hbm, wg),
                (wo_hbm, wo),
                (wc_hbm, wc),
                (atom_hbm, atoms.at[:, pl.ds(reach, atom_dev)]),
                (abias_hbm, abias_in),
                (ak_hbm, w_kv.at[:, pl.ds(0, atom_width)]),
                (av_hbm, w_kv.at[:, pl.ds(atom_width, atom_width)]),
                (aq_hbm, w_qg.at[:, pl.ds(0, atom_width)]),
                (ag_hbm, w_qg.at[:, pl.ds(atom_width, atom_width)]),
                (ao_hbm, w_ao),
            )
        )
    ]
    for load in loads:
        load.start()

    barrier = pltpu.get_barrier_semaphore()

    for offset in others:
        pl.semaphore_signal(
            barrier, inc=1, device_id=device_of(*peer(*offset)), device_id_type=MESH
        )
    for step in (1, -1):
        pl.semaphore_signal(barrier, inc=1, device_id=ring_device(step), device_id_type=MESH)
    for step in (1, -1, 2, -2):
        pl.semaphore_signal(barrier, inc=1, device_id=near(step), device_id_type=MESH)

    normed = norm(
        x_ref[...].astype(jnp.float32).reshape(flat, width), gain_ref[...].reshape(1, width)
    ).astype(jnp.bfloat16)
    loads[0].wait()
    key = jnp.dot(normed, wk[...], preferred_element_type=jnp.float32)
    loads[1].wait()
    value = jnp.dot(normed, wv[...], preferred_element_type=jnp.float32)
    loads[2].wait()
    query = jnp.dot(normed, wq[...], preferred_element_type=jnp.float32)

    spare = LANES - 2 * head_dim
    rest_dim = head_dim - spare
    lanes = lane_index((flat, LANES))
    row_lanes = lane_index((tokens, LANES))
    for head in range(heads):
        start = head * head_dim
        main = jnp.where(
            lanes < head_dim,
            placed_at(key, start, head_dim, 0),
            jnp.where(
                lanes < 2 * head_dim,
                placed_at(value, start, head_dim, head_dim),
                placed_at(query, start, spare, 2 * head_dim),
            ),
        )
        for core in range(2):
            below = jnp.zeros((tokens, LANES), jnp.float32)
            for s in range(per_core):
                first_row = (core * per_core + s) * tokens
                moved = placed_at(
                    query[first_row : first_row + tokens], start + spare, rest_dim, s * rest_dim
                )
                below = jnp.where(row_lanes // rest_dim == s, moved, below)
            qkv_send[core, head] = jnp.concatenate(
                [main[core * part : (core + 1) * part], below], axis=0
            ).astype(jnp.bfloat16)

    pl.semaphore_wait(barrier, peers + 5)
    my_slot = col * rows_plane + r4

    for offset in others:
        ylo, core, c = peer(*offset)
        pltpu.make_async_remote_copy(
            src_ref=qkv_send.at[core, ylo * n_col + c],
            dst_ref=qkv_recv.at[my_slot],
            send_sem=a2a_send_sem.at[0],
            recv_sem=a2a_recv_sem.at[0],
            device_id=device_of(ylo, core, c),
            device_id_type=MESH,
        ).start()
    qkv_recv[my_slot] = qkv_send[my_core, my_head]

    loads[3].wait()
    columns = bias_in.shape[2]
    flat_bias = bias_in[...].astype(jnp.float32).reshape(queries * tokens, columns)
    for tile in range(columns // LANES):
        bias_f[tile] = flat_bias[:, tile * LANES : (tile + 1) * LANES]
    rho = lax.broadcasted_iota(jnp.int32, (columns, columns), 0)
    lam = lane_index((columns, columns))
    ylo, rest = rho // (columns // 2), rho % (columns // 2)
    hd, rest = rest // (planes * 2), rest % (planes * 2)
    pz, core = rest // 2, rest % 2
    source = ((pz * 2 + ylo) * 2 + core) * heads + hd
    order = (lam == source).astype(jnp.bfloat16)
    low = lane_index((columns // 2, LANES)) < queries
    for j in range(tokens // 2):
        two = jnp.concatenate(
            [
                jnp.concatenate(
                    [
                        bias_f[tile, pl.ds(j + jj * (tokens // 2), queries, stride=tokens), :]
                        for tile in range(columns // LANES)
                    ],
                    axis=1,
                )
                for jj in range(2)
            ],
            axis=0,
        ).astype(jnp.bfloat16)
        moved = lax.dot_general(
            order, two, (((1,), (1,)), ((), ())), preferred_element_type=jnp.float32
        )
        top, bottom = moved[: columns // 2], moved[columns // 2 :]
        bias_t[pl.ds(j, columns // 2, stride=tokens), :] = jnp.where(
            low, top, pltpu.roll(bottom, queries, 1)
        )
        bias_t[pl.ds(j + tokens // 2, columns // 2, stride=tokens), :] = jnp.where(
            low, pltpu.roll(top, queries, 1), bottom
        )
    piece = planes * 2 * tokens
    bias_send[...] = bias_t[...].astype(jnp.bfloat16).reshape(heads, piece, LANES)


    near_sends = [
        near_copy(
            atom_hbm.at[:, pl.ds(atom_dev - reach, reach)], atoms.at[:, pl.ds(0, reach)], 1, 0
        ),
        near_copy(
            atom_hbm.at[:, pl.ds(0, reach)], atoms.at[:, pl.ds(reach + atom_dev, reach)], -1, 1
        ),
        near_copy(token_ref, token_rim.at[0], 1, 2),
        near_copy(token_ref, token_rim.at[1], -1, 3),
    ]
    for copy in near_sends:
        copy.start()


    def wait_some(buffer, count, sem):
        view = buffer.at[pl.ds(0, count)]
        pltpu.make_async_copy(view, view, sem).wait()

    eye_rows = lax.broadcasted_iota(jnp.int32, (2 * head_dim, LANES), 0)
    eye = (eye_rows == lane_index((2 * head_dim, LANES))).astype(jnp.bfloat16)

    def sample_rows(s):
        rows = qkv_recv[:, s * tokens // 16 * 16 : s * tokens // 16 * 16 + 16, :]
        return rows.astype(jnp.float32)[:, s * tokens % 16 : s * tokens % 16 + tokens, :]

    def transpose(s):
        kv_ring[z, s] = lax.dot_general(
            eye,
            sample_rows(s).reshape(plane_tokens, LANES).astype(jnp.bfloat16),
            (((1,), (1,)), ((), ())),
            preferred_element_type=jnp.float32,
        ).astype(jnp.bfloat16)

    def by_row(blocks):
        return jnp.concatenate(
            [blocks[c * rows_plane + r] for r in range(rows_plane) for c in range(n_col)], axis=0
        )

    def ring_block(way, hop, s):
        back = -hop if way == 0 else hop
        block = lax.rem(z + back + planes, planes)
        if hop < half_ring:
            return kv_ring.at[block, s]
        return kv_ring.at[block, s, pl.ds(way * head_dim, head_dim)]

    def ring_send(way, hop, s):
        back = 1 - hop if way == 0 else hop - 1
        block = lax.rem(z + back + planes, planes)
        view = kv_ring.at[block, s]
        if hop == half_ring:
            view = kv_ring.at[block, s, pl.ds(way * head_dim, head_dim)]
        return pltpu.make_async_remote_copy(
            src_ref=view,
            dst_ref=view,
            send_sem=ring_send_sem.at[way, hop - 1, s],
            recv_sem=ring_recv_sem.at[way, hop - 1, s],
            device_id=ring_device(1 if way == 0 else -1),
            device_id_type=MESH,
        )

    def ring_wait(way, hop, s):
        view = ring_block(way, hop, s)
        pltpu.make_async_copy(view, view, ring_recv_sem.at[way, hop - 1, s]).wait()

    log2e = math.log2(math.e)
    factor = log2e / math.sqrt(head_dim)

    sibling = (row + 1 - 2 * my_core, col)
    bias_forward = pltpu.make_async_remote_copy(
        src_ref=bias_recv.at[my_core],
        dst_ref=bias_recv.at[my_core],
        send_sem=near_send_sem.at[8],
        recv_sem=near_recv_sem.at[8],
        device_id=sibling,
        device_id_type=MESH,
    )

    def bias_pass():
        wait_some(bias_recv.at[my_core], heads - 1, a2a_recv_sem.at[1])
        bias_forward.start()

    def bias_stage():
        bias_forward.wait_recv()
        half_lanes = lane_index((piece, LANES)) < queries
        for c in range(n_col):
            for pair in range(rows_plane // 2):
                even = bias_recv[0, pair * n_col + c].astype(jnp.float32)
                odd = bias_recv[1, pair * n_col + c].astype(jnp.float32)
                for y, merged in enumerate(
                    (
                        jnp.where(half_lanes, even, pltpu.roll(odd, queries, 1)),
                        jnp.where(half_lanes, pltpu.roll(even, queries, 1), odd),
                    )
                ):
                    bias_keys[:, c, y, :, pair * LANES : (pair + 1) * LANES] = merged.astype(
                        jnp.bfloat16
                    ).reshape(planes, 2 * tokens, LANES)
        eye_row = lax.broadcasted_iota(jnp.int32, (plane_tokens, plane_tokens), 0)
        eye_q = (eye_row == lane_index((plane_tokens, plane_tokens))).astype(jnp.bfloat16)
        for zz in range(planes):
            block = bias_keys[zz].reshape(plane_tokens, plane_tokens)
            bias_all[zz] = (
                lax.dot_general(
                    eye_q, block, (((1,), (1,)), ((), ())), preferred_element_type=jnp.float32
                )
                * log2e
            )

    def atom_setup():
        for load in loads[7:]:
            load.wait()
        for copy in near_sends:
            copy.wait_recv()
        base = (device - 2) * tokens
        ids = lax.broadcasted_iota(jnp.int32, (atom_dev, atom_dev), 0)
        eye_a = (ids == lane_index((atom_dev, atom_dev))).astype(jnp.bfloat16)
        chosen = []
        for own, first_atom, count in (
            (token_rim[0], atom_dev - reach, reach),
            (token_ref[...], 0, atom_dev),
            (token_rim[1], 0, reach),
        ):
            hit = ((own - base) == ids).astype(jnp.bfloat16)
            across = lax.dot_general(
                eye_a, hit, (((1,), (1,)), ((), ())), preferred_element_type=jnp.float32
            )
            chosen.append(across[first_atom : first_atom + count])
        selector[...] = jnp.concatenate(chosen, axis=0).astype(jnp.bfloat16)
        for w in range(windows):
            place = device * atom_dev + w * WQ - reach + lane_index((WQ, WK))
            valid = (place >= 0) & (place < devices * atom_dev)
            rows = abias_in[w].astype(jnp.float32)
            for h in range(atom_heads):
                abias[w, h * WQ : (h + 1) * WQ, :] = jnp.where(
                    valid, rows[:, h * WK : (h + 1) * WK] * log2e, -1e9
                )

    def weight_product():
        loads[5].wait()
        loads[6].wait()
        product = jnp.dot(wo[...], wc[...], preferred_element_type=jnp.float32)
        high = product.astype(jnp.bfloat16)
        w_oc[0] = high
        w_oc[1] = (product - high.astype(jnp.float32)).astype(jnp.bfloat16)

    def attend(s):
        below = qkv_recv[:, part - tokens :, :].astype(jnp.float32)[:, tokens:, :]
        q_lanes = lane_index((plane_tokens, LANES))
        q_one = jnp.where(
            q_lanes < spare,
            rolled(by_row(sample_rows(s)), spare),
            rolled(by_row(below), spare - s * rest_dim),
        ).astype(jnp.bfloat16)[:, :head_dim]
        peak = None
        for zz in range(planes):
            raw = jnp.dot(q_one, kv_ring[zz, s, :head_dim, :], preferred_element_type=jnp.float32)
            score = raw * factor + bias_all[zz]
            scores[zz] = score
            peak = score if peak is None else jnp.maximum(peak, score)
        peak = jnp.max(peak, axis=-1, keepdims=True)
        total = None
        ones = jnp.ones((LANES - head_dim, plane_tokens), jnp.bfloat16)
        for zz in range(planes):
            weights = jnp.exp2(scores[zz] - peak).astype(jnp.bfloat16)
            v_one = jnp.concatenate([kv_ring[zz, s, head_dim:, :], ones], axis=0)
            mixed = lax.dot_general(
                weights, v_one, (((1,), (1,)), ((), ())), preferred_element_type=jnp.float32
            )
            total = mixed if total is None else total + mixed
        attended = total / total[:, head_dim : head_dim + 1]
        out_f[s] = attended

    def hops(hop, *wanted):
        for s in wanted:
            for way in range(2):
                ring_wait(way, hop, s)
                if hop < half_ring:
                    ring_send(way, hop + 1, s).start()

    def own(*wanted):
        for s in wanted:
            transpose(s)
            for way in range(2):
                ring_send(way, 1, s).start()

    wait_some(qkv_recv, peers - 1, a2a_recv_sem.at[0])
    split = (per_core + 1) // 2
    early, late = range(split), range(split, per_core)
    own(*range(per_core))
    for offset in others:
        if offset[1] == 0:
            ylo, core, c = peer(*offset)
            pltpu.make_async_remote_copy(
                src_ref=bias_send.at[ylo * n_col + c],
                dst_ref=bias_recv.at[my_core, my_head],
                send_sem=a2a_send_sem.at[1],
                recv_sem=a2a_recv_sem.at[1],
                device_id=device_of(ylo, core, c),
                device_id_type=MESH,
            ).start()
    bias_recv[my_core, my_head] = bias_send[my_head]

    loads[4].wait()
    gate_s[...] = jnp.dot(normed, wg[...], preferred_element_type=jnp.float32).astype(jnp.bfloat16)
    hops(1, *early)
    atom_setup()
    hops(1, *late)
    hops(2, *early)
    bias_pass()
    hops(2, *late)
    weight_product()
    hops(3, *early)
    bias_stage()
    hops(3, *late)
    for s in early:
        hops(half_ring, s)
        attend(s)
    for s in late:
        hops(half_ring, s)
        attend(s)

    wide = lane_index((plane_tokens, LANES))
    outs = [out_f[s] for s in range(per_core)]
    upper = jnp.where(
        wide < head_dim,
        outs[0],
        jnp.where(wide < 2 * head_dim, rolled(outs[1], head_dim), rolled(outs[4], 2 * head_dim)),
    )
    lower = jnp.where(
        wide < head_dim,
        outs[2],
        jnp.where(
            wide < 2 * head_dim, rolled(outs[3], head_dim), rolled(outs[4], 2 * head_dim - spare)
        ),
    )
    out_send[...] = jnp.concatenate(
        [one.reshape(peers, tokens, LANES) for one in (upper, lower)], axis=1
    ).astype(jnp.bfloat16)
    my_place = my_core * heads + my_head

    for offset in others:
        ylo, core, c = peer(*offset)
        pltpu.make_async_remote_copy(
            src_ref=out_send.at[(ylo * 2 + core) * n_col + c],
            dst_ref=out_recv.at[my_place],
            send_sem=a2a_send_sem.at[2],
            recv_sem=a2a_recv_sem.at[2],
            device_id=device_of(ylo, core, c),
            device_id_type=MESH,
        ).start()
    out_recv[my_place] = out_send[me]

    wait_some(out_recv, peers - 1, a2a_recv_sem.at[2])
    tiles = [None] * (width // LANES)
    for head in range(heads):
        pieces = []
        for core in range(2):
            both = out_recv[core * heads + head].astype(jnp.float32)
            upper, lower = both[:tokens], both[tokens:]
            pieces += [
                upper,
                rolled(upper, -head_dim),
                lower,
                rolled(lower, -head_dim),
                jnp.where(
                    row_lanes < spare,
                    rolled(upper, -2 * head_dim),
                    rolled(lower, spare - 2 * head_dim),
                ),
            ]
        piece_rows = jnp.concatenate(pieces, axis=0)
        tile, rest = divmod(head * head_dim, LANES)
        moved = rolled(piece_rows, rest)
        tiles[tile] = moved if tiles[tile] is None else jnp.where(lanes >= rest, moved, tiles[tile])
        if rest + head_dim > LANES:
            tiles[tile + 1] = moved
    attended = jnp.concatenate(tiles, axis=1)
    gated = (attended * jax.nn.sigmoid(gate_s[...].astype(jnp.float32))).astype(jnp.bfloat16)
    cond = jnp.dot(gated, w_oc[0], preferred_element_type=jnp.float32) + jnp.dot(
        gated, w_oc[1], preferred_element_type=jnp.float32
    )
    cond_rim[2] = cond.astype(jnp.bfloat16)
    cond_sends = [
        near_copy(cond_rim.at[2], cond_rim.at[1], 1, 4),
        near_copy(cond_rim.at[2], cond_rim.at[0], 2, 5),
        near_copy(cond_rim.at[2], cond_rim.at[3], -1, 6),
    ]
    for copy in cond_sends:
        copy.start()
    update = jnp.dot(gated, wo[...], preferred_element_type=jnp.float32)
    update_ref[...] = update.reshape(samples, tokens, width).astype(jnp.bfloat16)
    for copy in cond_sends:
        copy.wait_recv()

    conds = [
        cond_rim[b].astype(jnp.float32).reshape(samples, tokens, atom_width) for b in range(4)
    ]
    chooser = selector[:, : 4 * tokens]
    atom_gain = again_ref[...].reshape(1, atom_width)
    shares = jnp.full((2 * atom_width, atom_width), 1.0 / atom_width, jnp.bfloat16)

    def row_mean(rows):
        high = rows.astype(jnp.bfloat16)
        low = (rows - high.astype(jnp.float32)).astype(jnp.bfloat16)
        return jnp.dot(
            jnp.concatenate([high, low], axis=1), shares, preferred_element_type=jnp.float32
        )

    for s in range(samples):
        near_cond = jnp.concatenate([conds[b][s] for b in range(4)], axis=0).astype(jnp.bfloat16)
        carried = jnp.dot(chooser, near_cond, preferred_element_type=jnp.float32)
        state = atoms[s].astype(jnp.float32) + carried
        own_state = state[reach : reach + atom_dev]
        state_s[s] = own_state
        center = state - row_mean(state)
        spread = row_mean(center * center)
        atom_normed = (center * lax.rsqrt(spread + EPSILON) * atom_gain).astype(jnp.bfloat16)
        kv_s[s] = jnp.dot(atom_normed, w_kv[...], preferred_element_type=jnp.float32).astype(
            jnp.bfloat16
        )
        qg_s[s] = jnp.dot(
            atom_normed[reach : reach + atom_dev], w_qg[...], preferred_element_type=jnp.float32
        ).astype(jnp.bfloat16)

    atom_factor = log2e / math.sqrt(atom_hdim)
    head_lane = lane_index((WQ, atom_width)) // atom_hdim
    ones_key = jnp.ones((WK, atom_width), jnp.bfloat16)
    two_lane = lane_index((WQ, 2 * atom_width)) // atom_hdim % atom_heads

    def atom_attend(s):
        raws, mixes = [], []
        for w in range(windows):
            q_rows = qg_s[s, w * WQ : (w + 1) * WQ, :atom_width].astype(jnp.float32)
            spread_q = jnp.concatenate(
                [jnp.where(head_lane == h, q_rows, 0.0) for h in range(atom_heads)], axis=0
            ).astype(jnp.bfloat16)
            k_rows = kv_s[s, w * WQ : w * WQ + WK, :atom_width]
            raws.append(
                lax.dot_general(
                    spread_q, k_rows, (((1,), (1,)), ((), ())), preferred_element_type=jnp.float32
                )
            )
        for w in range(windows):
            score = raws[w] * atom_factor + abias[w]
            weights = jnp.exp2(score - jnp.max(score, axis=-1, keepdims=True))
            v_rows = kv_s[s, w * WQ : w * WQ + WK, atom_width:]
            mixes.append(
                jnp.dot(
                    weights.astype(jnp.bfloat16),
                    jnp.concatenate([v_rows, ones_key], axis=1),
                    preferred_element_type=jnp.float32,
                )
            )
        for w in range(windows):
            joined = mixes[w][:WQ]
            for h in range(1, atom_heads):
                joined = jnp.where(two_lane == h, mixes[w][h * WQ : (h + 1) * WQ], joined)
            gate = qg_s[s, w * WQ : (w + 1) * WQ, atom_width:].astype(jnp.float32)
            gated_s[s, w * WQ : (w + 1) * WQ, :] = (
                joined[:, :atom_width] / joined[:, atom_width:] * jax.nn.sigmoid(gate)
            ).astype(jnp.bfloat16)

    def atom_step(i, carry):
        for half in range(2):
            atom_attend(2 * i + half)
        return carry

    lax.fori_loop(0, samples // 2, atom_step, 0)

    local = token_ref[...] - (device - 1) * tokens
    gather = (local == lax.broadcasted_iota(jnp.int32, (2 * tokens, atom_dev), 0)).astype(
        jnp.bfloat16
    )
    sums = []
    for s in range(samples):
        result = (
            state_s[s] + jnp.dot(gated_s[s], w_ao[...], preferred_element_type=jnp.float32)
        ).astype(jnp.bfloat16)
        result_ref[s] = result
        sums.append(jnp.dot(gather, result, preferred_element_type=jnp.float32))
    pool_send[...] = jnp.concatenate([one[:tokens] for one in sums], axis=0).astype(jnp.bfloat16)
    pool_copy = near_copy(pool_send, pool_recv, -1, 7)
    pool_copy.start()
    pool_copy.wait_recv()
    arrived = jnp.where(device < devices - 1, pool_recv[...].astype(jnp.float32), 0.0)
    own_sums = jnp.concatenate([one[tokens:] for one in sums], axis=0) + arrived
    sums_ref[...] = own_sums
    for copy in near_sends + cond_sends + [pool_copy, bias_forward]:
        copy.wait_send()
    wait_some(qkv_recv, peers - 1, a2a_send_sem.at[0])
    wait_some(bias_send, heads - 1, a2a_send_sem.at[1])
    wait_some(out_recv, peers - 1, a2a_send_sem.at[2])

    def drain(s, carry):
        for way in range(2):
            for hop in range(1, half_ring + 1):
                ring_send(way, hop, s).wait_send()
        return carry

    lax.fori_loop(0, per_core, drain, 0)


def finish_kernel(sums_ref, gain_ref, weight_ref, update_in, result_in, update, result, pool):
    pooled = norm(sums_ref[...], gain_ref[...].reshape(1, -1)).astype(jnp.bfloat16)
    token_pool = jnp.dot(pooled, weight_ref[...], preferred_element_type=jnp.float32)
    pool[...] = token_pool.reshape(pool.shape).astype(jnp.bfloat16)
    update[...] = update_in[...]
    result[...] = result_in[...]


def diffusion_pass(
    single, pair_bias, token_gain, w_query, w_key, w_value, w_gate, w_out, w_cond, atom_single,
    atom_token, atom_bias, atom_gain, atom_query, atom_key, atom_value, atom_gate, atom_out,
    pool_gain, w_pool, n_row, n_col
):
    samples, tokens, width = single.shape
    queries, _, columns = pair_bias.shape
    heads = columns // n_row
    head_dim = width // heads
    rows_plane = 2 * heads // n_col
    planes = n_row // rows_plane
    peers = rows_plane * n_col
    per_core = samples // 2
    plane_tokens = peers * tokens
    padded = -(-per_core * tokens // 16) * 16
    piece = planes * 2 * tokens
    _, atom_dev, atom_width = atom_single.shape
    reach = (WK - WQ) // 2
    ext = atom_dev + 2 * reach
    windows = atom_dev // WQ
    atom_heads = atom_bias.shape[2] // WK
    bf16, f32 = jnp.bfloat16, jnp.float32
    vmem = pl.BlockSpec(memory_space=pltpu.VMEM)
    anywhere = pl.BlockSpec(memory_space=pl.ANY)
    update, result, sums = pl.pallas_call(
        functools.partial(pass_kernel, heads, rows_plane, planes, n_col),
        out_shape=(
            jax.ShapeDtypeStruct((samples, tokens, width), bf16),
            jax.ShapeDtypeStruct(atom_single.shape, bf16),
            jax.ShapeDtypeStruct((samples * tokens, atom_width), f32),
        ),
        in_specs=[vmem, vmem]
        + [anywhere] * 8
        + [vmem, anywhere, vmem]
        + [anywhere] * 5,
        out_specs=(vmem, vmem, vmem),
        scratch_shapes=[
            pltpu.VMEM(pair_bias.shape, bf16),
            pltpu.VMEM(w_query.shape, bf16),
            pltpu.VMEM(w_key.shape, bf16),
            pltpu.VMEM(w_value.shape, bf16),
            pltpu.VMEM(w_gate.shape, bf16),
            pltpu.VMEM(w_out.shape, bf16),
            pltpu.VMEM(w_cond.shape, bf16),
            pltpu.VMEM((columns // LANES, queries * tokens, LANES), f32),
            pltpu.VMEM((heads * piece, LANES), f32),
            pltpu.VMEM((heads, piece, LANES), bf16),
            pltpu.VMEM((2, heads, piece, LANES), bf16),
            pltpu.VMEM((planes, n_col, 2, 2 * tokens, plane_tokens), bf16),
            pltpu.VMEM((planes, plane_tokens, plane_tokens), f32),
            pltpu.VMEM((2, heads, padded, LANES), bf16),
            pltpu.VMEM((peers, padded, LANES), bf16),
            pltpu.VMEM((planes, per_core, 2 * head_dim, plane_tokens), bf16),
            pltpu.VMEM((planes, plane_tokens, plane_tokens), f32),
            pltpu.VMEM((per_core, plane_tokens, LANES), f32),
            pltpu.VMEM((peers, 2 * tokens, LANES), bf16),
            pltpu.VMEM((peers, 2 * tokens, LANES), bf16),
            pltpu.VMEM((samples * tokens, width), bf16),
            pltpu.VMEM((2,) + w_cond.shape, bf16),
            pltpu.VMEM((samples, ext, atom_width), bf16),
            pltpu.VMEM((2, 1, atom_dev), jnp.int32),
            pltpu.VMEM(atom_bias.shape, bf16),
            pltpu.VMEM((windows, atom_heads * WQ, WK), f32),
            pltpu.VMEM((atom_width, 2 * atom_width), bf16),
            pltpu.VMEM((atom_width, 2 * atom_width), bf16),
            pltpu.VMEM(atom_out.shape, bf16),
            pltpu.VMEM((ext, atom_dev), bf16),
            pltpu.VMEM((4, samples * tokens, atom_width), bf16),
            pltpu.VMEM((samples, atom_dev, atom_width), f32),
            pltpu.VMEM((samples, ext, 2 * atom_width), bf16),
            pltpu.VMEM((samples, atom_dev, 2 * atom_width), bf16),
            pltpu.VMEM((samples, atom_dev, atom_width), bf16),
            pltpu.VMEM((samples * tokens, atom_width), bf16),
            pltpu.VMEM((samples * tokens, atom_width), bf16),
            pltpu.SemaphoreType.DMA((14,)),
            pltpu.SemaphoreType.DMA((3,)),
            pltpu.SemaphoreType.DMA((3,)),
            pltpu.SemaphoreType.DMA((2, planes // 2, per_core)),
            pltpu.SemaphoreType.DMA((2, planes // 2, per_core)),
            pltpu.SemaphoreType.DMA((9,)),
            pltpu.SemaphoreType.DMA((9,)),
        ],
        compiler_params=pltpu.CompilerParams(
            collective_id=1, has_side_effects=True, vmem_limit_bytes=56 * 1024 * 1024
        ),
    )(
        single,
        token_gain,
        pair_bias,
        w_query,
        w_key,
        w_value,
        w_gate,
        w_out,
        w_cond,
        atom_single,
        atom_token.reshape(1, atom_dev),
        atom_bias,
        atom_gain,
        atom_query,
        atom_key,
        atom_value,
        atom_gate,
        atom_out,
    )
    return pl.pallas_call(
        finish_kernel,
        out_shape=(
            jax.ShapeDtypeStruct(update.shape, bf16),
            jax.ShapeDtypeStruct(result.shape, bf16),
            jax.ShapeDtypeStruct((samples, tokens, width), bf16),
        ),
        in_specs=[vmem] * 5,
        out_specs=(vmem, vmem, vmem),
        compiler_params=pltpu.CompilerParams(vmem_limit_bytes=56 * 1024 * 1024),
    )(sums, pool_gain, w_pool, update, result)


def solution(mesh):
    n_row, n_col = mesh.shape["row"], mesh.shape["col"]

    def on_device(*arrays):
        return diffusion_pass(*arrays, n_row, n_col)

    placed = (
        P(None, ("row", "col"), None),
        P("row", "col", None),
        P(),
        P(),
        P(),
        P(),
        P(),
        P(),
        P(),
        P(None, ("row", "col"), None),
        P(("row", "col")),
        P(("row", "col"), None, None),
        P(),
        P(),
        P(),
        P(),
        P(),
        P(),
        P(),
        P(),
    )
    return jax.shard_map(
        on_device,
        mesh=mesh,
        in_specs=placed,
        out_specs=(
            P(None, ("row", "col"), None),
            P(None, ("row", "col"), None),
            P(None, ("row", "col"), None),
        ),
        check_vma=False,
    )
```

time: 99.5 us -> 75.4 us (0.76)
  Pallas kernels: 92.5 us -> 74.7 us
  local copies, waits for them, and re-layouts: 6.1 us -> 0 us
    pallas_call x1, Pallas kernels: 92.5 us -> 72.5 us  [diffusion_pass(): pl.pallas_call(functools.partial(pass_kernel, heads, rows_plane, planes,...]
    unnamed x3 -> x0, local copies, waits for them, and re-layouts: 4.84 us -> none
    pallas_call x0 -> x1, Pallas kernels: none -> 2.18 us  [diffusion_pass(): pl.pallas_call(finish_kernel, out_shape=(jax.ShapeDtypeStruct(update.shap...]
    reshape x1 -> x0, local copies, waits for them, and re-layouts: 1.27 us -> none  [diffusion_pass(): token_gain.reshape(1, width)]
where the time goes in v3:
time: 75.4 us; the launch traced here: 75.3 us
  Pallas kernels  74.7 us (99%)
    pallas_call x1, Pallas kernels, diffusion_pass(): pl.pallas_call(functools.partial(pass_kernel, heads, rows_plane, planes,...  72.5 us
    pallas_call x1, Pallas kernels, diffusion_pass(): pl.pallas_call(finish_kernel, out_shape=(jax.ShapeDtypeStruct(update.shap...  2.18 us

profile of v3, /device:TPU:6, one launch (start us, length us, event | category | flops | bytes accessed | tf_op | source)
XLA Modules:
  0.0 75.3 jit_solution(2688215139887437846)
XLA Ops:
  0.6 72.5 %shard_map.211 = (bf16[10,8,768]{2,1,0:T(8,128)(2,1)}, bf16[10,128,128]{2,1,0:T(8,128)(2,1)}, f32[80,128]{1,0:T(8,128)}) custom-call(bf16[10,8,768]{2,1,0:T(8,128)(2,1)} %x_ref.1, f32[768]{0:T(1024)} %gain_ref.2, bf16[64,8,512]{2,1,0:T(8,128)(2,1)} %bias_hbm.1, bf16[768,768]{1,0:T(8,128)(2,1)} %wq_hbm.1, bf16[768,768]{1,0:T(8,128)(2,1)} %wk_hbm.1, ...), custom_call_target="tpu_custom_call" | custom-call | tf_op jit(solution)/shard_map/pallas_call | solution.py:736
  73.1 2.2 %shard_map.212 = (bf16[10,8,768]{2,1,0:T(8,128)(2,1)}, bf16[10,128,128]{2,1,0:T(8,128)(2,1)}, bf16[10,8,768]{2,1,0:T(8,128)(2,1)}) custom-call(f32[80,128]{1,0:T(8,128)} %get-tuple-element.6.sums_ref, f32[128]{0:T(128)} %gain_ref.3, bf16[128,768]{1,0:T(8,128)(2,1)} %weight_ref.1, bf16[10,8,768]{2,1,0:T(8,128)(2,1)} %get-tuple-element.7.update_in, ...), custom_call_target="tpu_custom_call" | custom-call | tf_op jit(solution)/shard_map/pallas_call | solution.py:817

commit v4 on v3

--- a/solution.py
+++ b/solution.py
@@ -83,9 +83,14 @@
     kv_ring,
     scores,
     out_f,
-    out_send,
-    out_recv,
-    gate_s,
+    early_send,
+    early_recv,
+    late_send,
+    late_recv,
+    gate_send,
+    gate_recv,
+    own_early,
+    own_late,
     w_oc,
     atoms,
     token_rim,
@@ -95,7 +100,6 @@
     w_qg,
     w_ao,
     selector,
-    cond_rim,
     state_s,
     kv_s,
     qg_s,
@@ -107,6 +111,7 @@
     a2a_recv_sem,
     ring_send_sem,
     ring_recv_sem,
+    edge_send_sem,
     near_send_sem,
     near_recv_sem,
 ):
@@ -206,6 +211,24 @@
     for step in (1, -1, 2, -2):
         pl.semaphore_signal(barrier, inc=1, device_id=near(step), device_id_type=MESH)
 
+    def greet_plane(step):
+        other = lax.rem(z + step + planes, planes)
+        for p in range(peers):
+            pl.semaphore_signal(
+                barrier,
+                inc=1,
+                device_id=(other * rows_plane + p // n_col, p % n_col),
+                device_id_type=MESH,
+            )
+
+    @pl.when(me < 2)
+    def _():
+        greet_plane(-1)
+
+    @pl.when(me == peers - 1)
+    def _():
+        greet_plane(1)
+
     normed = norm(
         x_ref[...].astype(jnp.float32).reshape(flat, width), gain_ref[...].reshape(1, width)
     ).astype(jnp.bfloat16)
@@ -243,7 +266,7 @@
                 [main[core * part : (core + 1) * part], below], axis=0
             ).astype(jnp.bfloat16)
 
-    pl.semaphore_wait(barrier, peers + 5)
+    pl.semaphore_wait(barrier, peers + 8)
     my_slot = col * rows_plane + r4
 
     for offset in others:
@@ -257,6 +280,23 @@
             device_id_type=MESH,
         ).start()
     qkv_recv[my_slot] = qkv_send[my_core, my_head]
+
+    loads[4].wait()
+    gate = jnp.dot(normed, wg[...], preferred_element_type=jnp.float32)
+    for head in range(heads):
+        left = placed_at(gate, head * head_dim, head_dim, 0)
+        right = placed_at(gate, head * head_dim, head_dim, head_dim)
+        for core in range(2):
+            rows = []
+            for s in range(0, per_core, 2):
+                first_row = (core * per_core + s) * tokens
+                one = left[first_row : first_row + tokens]
+                if s + 1 < per_core:
+                    beside = right[first_row + tokens : first_row + 2 * tokens]
+                    one = jnp.where(row_lanes < head_dim, one, beside)
+                rows.append(one)
+            rows.append(jnp.zeros((tokens, LANES), jnp.float32))
+            gate_send[core, head] = jnp.concatenate(rows, axis=0).astype(jnp.bfloat16)
 
     loads[3].wait()
     columns = bias_in.shape[2]
@@ -469,25 +509,172 @@
             )
             total = mixed if total is None else total + mixed
         attended = total / total[:, head_dim : head_dim + 1]
-        out_f[s] = attended
-
-    def hops(hop, *wanted):
-        for s in wanted:
+        gate_rows = gate_recv[:, s // 4 * 16 : s // 4 * 16 + 16, :].astype(jnp.float32)
+        first_row = s // 2 * tokens % 16
+        gate = rolled(by_row(gate_rows[:, first_row : first_row + tokens, :]), -(s % 2) * head_dim)
+        out_f[s] = attended * jax.nn.sigmoid(gate)
+
+    steps = [(1, 0), (1, 1), (1, 2), (2, 0), (2, 1), (2, 2), (3, 0), (3, 1), (1, 3), (3, 2)]
+    steps += [(4, 0), (1, 4), (4, 1), (2, 3), (4, 2), (2, 4), (3, 3), (3, 4), (4, 3), (4, 4)]
+    in_flight = 4
+
+    def settle(hop, s):
+        for way in range(2):
+            ring_send(way, hop, s).wait_send()
+
+    def ring_steps(first, last):
+        for k in range(first, last):
+            hop, s = steps[k]
+            if hop == 1:
+                transpose(s)
             for way in range(2):
-                ring_wait(way, hop, s)
-                if hop < half_ring:
-                    ring_send(way, hop + 1, s).start()
-
-    def own(*wanted):
-        for s in wanted:
-            transpose(s)
+                if hop > 1:
+                    ring_wait(way, hop - 1, s)
+            if k >= in_flight:
+                settle(*steps[k - in_flight])
             for way in range(2):
-                ring_send(way, 1, s).start()
+                ring_send(way, hop, s).start()
+
+    def complete(s):
+        for way in range(2):
+            ring_wait(way, half_ring, s)
+
+    wide = lane_index((plane_tokens, LANES))
+    my_place = my_core * heads + my_head
+    edges = [
+        (place, (lax.rem(z + step + planes, planes) * rows_plane + p // n_col, p % n_col))
+        for place, step, p in ((-1, -1, peers - 1), (peers, 1, 0), (peers + 1, 1, 1))
+    ]
+
+    def result_copies(piece_of, target, which):
+        plane_copies, edge_copies = [], []
+        for offset in others:
+            ylo, core, c = peer(*offset)
+            plane_copies.append(
+                pltpu.make_async_remote_copy(
+                    src_ref=piece_of((ylo * 2 + core) * n_col + c),
+                    dst_ref=target.at[0, my_place],
+                    send_sem=a2a_send_sem.at[which],
+                    recv_sem=a2a_recv_sem.at[which],
+                    device_id=device_of(ylo, core, c),
+                    device_id_type=MESH,
+                )
+            )
+        for i, (place, other) in enumerate(edges):
+            edge_copies.append(
+                pltpu.make_async_remote_copy(
+                    src_ref=piece_of(place),
+                    dst_ref=target.at[1, my_place],
+                    send_sem=edge_send_sem.at[which - 2, i],
+                    recv_sem=a2a_recv_sem.at[which + 2],
+                    device_id=other,
+                    device_id_type=MESH,
+                )
+            )
+        return plane_copies, edge_copies
+
+    def early_piece(place):
+        return early_send.at[place + 1]
+
+    def late_piece(place):
+        return late_send.at[place + 1]
+
+    early_copies = result_copies(early_piece, early_recv, 2)
+    late_copies = result_copies(late_piece, late_recv, 3)
+
+    def padded_rows(rows):
+        blank = jnp.zeros((3 * tokens, LANES), jnp.float32)
+        return jnp.concatenate([blank, rows, blank], axis=0)
+
+    def send_early():
+        pair = padded_rows(jnp.where(wide < head_dim, out_f[0], rolled(out_f[1], head_dim)))
+        third = padded_rows(out_f[2])
+        beside = rolled(third, head_dim)
+        for place in range(peers + 3):
+            start = place * tokens
+            rows = [pair[start : start + 4 * tokens]]
+            for first in (start, start + 2 * tokens):
+                rows.append(
+                    jnp.where(
+                        row_lanes < head_dim,
+                        third[first : first + tokens],
+                        beside[first + tokens : first + 2 * tokens],
+                    )
+                )
+            early_send[place] = jnp.concatenate(rows, axis=0).astype(jnp.bfloat16)
+        for copy in early_copies[0] + early_copies[1]:
+            copy.start()
+        early_recv[0, my_place] = early_send[me + 1]
+
+    def send_late():
+        both = jnp.where(wide < head_dim, out_f[3], rolled(out_f[4], head_dim))
+        rows = padded_rows(both)
+        for place in range(peers + 3):
+            late_send[place] = rows[place * tokens : (place + 4) * tokens].astype(jnp.bfloat16)
+        for copy in late_copies[0] + late_copies[1]:
+            copy.start()
+        late_recv[0, my_place] = late_send[me + 1]
+
+    def wait_results(target, which):
+        wait_some(target.at[0], peers - 1, a2a_recv_sem.at[which])
+
+        @pl.when((me < 2) | (me == peers - 1))
+        def _():
+            wait_some(target.at[1], peers, a2a_recv_sem.at[which + 2])
+
+    chosen_buffer = [
+        jnp.where(me < 2, 1, 0),
+        jnp.where(me < 1, 1, 0),
+        0,
+        jnp.where(me == peers - 1, 1, 0),
+    ]
+
+    def joined_rows(head_rows):
+        tiles = [None] * (width // LANES)
+        for head in range(heads):
+            rows = jnp.concatenate(
+                [
+                    one
+                    for block in range(4)
+                    for core in range(2)
+                    for one in head_rows(block, core * heads + head)
+                ],
+                axis=0,
+            )
+            tile, rest = divmod(head * head_dim, LANES)
+            moved = rolled(rows, rest)
+            if tiles[tile] is None:
+                tiles[tile] = moved
+            else:
+                tiles[tile] = jnp.where(lane_index(moved.shape) >= rest, moved, tiles[tile])
+            if rest + head_dim > LANES:
+                tiles[tile + 1] = moved
+        return jnp.concatenate(tiles, axis=1)
+
+    def early_rows(block, place):
+        rows = early_recv[chosen_buffer[block], place].astype(jnp.float32)
+        both = rows[block * tokens : (block + 1) * tokens]
+        third = rows[(4 + block // 2) * tokens : (5 + block // 2) * tokens]
+        return [both, rolled(both, -head_dim), rolled(third, -head_dim) if block % 2 else third]
+
+    def late_rows(block, place):
+        both = late_recv[chosen_buffer[block], place].astype(jnp.float32)
+        both = both[block * tokens : (block + 1) * tokens]
+        return [both, rolled(both, -head_dim)]
+
+    def condition(head_rows, members, own_rows):
+        gated = joined_rows(head_rows)
+        count = 2 * len(members) * tokens
+        own_rows[...] = gated[2 * count : 3 * count]
+        gated = gated.astype(jnp.bfloat16)
+        cond = jnp.dot(gated, w_oc[0], preferred_element_type=jnp.float32) + jnp.dot(
+            gated, w_oc[1], preferred_element_type=jnp.float32
+        )
+        return cond.reshape(4, 2, len(members), tokens, atom_width)
 
     wait_some(qkv_recv, peers - 1, a2a_recv_sem.at[0])
-    split = (per_core + 1) // 2
-    early, late = range(split), range(split, per_core)
-    own(*range(per_core))
+    early, late = range(3), range(3, per_core)
+    ring_steps(0, 3)
     for offset in others:
         if offset[1] == 0:
             ylo, core, c = peer(*offset)
@@ -500,102 +687,37 @@
                 device_id_type=MESH,
             ).start()
     bias_recv[my_core, my_head] = bias_send[my_head]
-
-    loads[4].wait()
-    gate_s[...] = jnp.dot(normed, wg[...], preferred_element_type=jnp.float32).astype(jnp.bfloat16)
-    hops(1, *early)
-    atom_setup()
-    hops(1, *late)
-    hops(2, *early)
-    bias_pass()
-    hops(2, *late)
-    weight_product()
-    hops(3, *early)
-    bias_stage()
-    hops(3, *late)
-    for s in early:
-        hops(half_ring, s)
-        attend(s)
-    for s in late:
-        hops(half_ring, s)
-        attend(s)
-
-    wide = lane_index((plane_tokens, LANES))
-    outs = [out_f[s] for s in range(per_core)]
-    upper = jnp.where(
-        wide < head_dim,
-        outs[0],
-        jnp.where(wide < 2 * head_dim, rolled(outs[1], head_dim), rolled(outs[4], 2 * head_dim)),
-    )
-    lower = jnp.where(
-        wide < head_dim,
-        outs[2],
-        jnp.where(
-            wide < 2 * head_dim, rolled(outs[3], head_dim), rolled(outs[4], 2 * head_dim - spare)
-        ),
-    )
-    out_send[...] = jnp.concatenate(
-        [one.reshape(peers, tokens, LANES) for one in (upper, lower)], axis=1
-    ).astype(jnp.bfloat16)
-    my_place = my_core * heads + my_head
-
     for offset in others:
         ylo, core, c = peer(*offset)
         pltpu.make_async_remote_copy(
-            src_ref=out_send.at[(ylo * 2 + core) * n_col + c],
-            dst_ref=out_recv.at[my_place],
-            send_sem=a2a_send_sem.at[2],
-            recv_sem=a2a_recv_sem.at[2],
+            src_ref=gate_send.at[core, ylo * n_col + c],
+            dst_ref=gate_recv.at[my_slot],
+            send_sem=a2a_send_sem.at[4],
+            recv_sem=a2a_recv_sem.at[6],
             device_id=device_of(ylo, core, c),
             device_id_type=MESH,
         ).start()
-    out_recv[my_place] = out_send[me]
-
-    wait_some(out_recv, peers - 1, a2a_recv_sem.at[2])
-    tiles = [None] * (width // LANES)
-    for head in range(heads):
-        pieces = []
-        for core in range(2):
-            both = out_recv[core * heads + head].astype(jnp.float32)
-            upper, lower = both[:tokens], both[tokens:]
-            pieces += [
-                upper,
-                rolled(upper, -head_dim),
-                lower,
-                rolled(lower, -head_dim),
-                jnp.where(
-                    row_lanes < spare,
-                    rolled(upper, -2 * head_dim),
-                    rolled(lower, spare - 2 * head_dim),
-                ),
-            ]
-        piece_rows = jnp.concatenate(pieces, axis=0)
-        tile, rest = divmod(head * head_dim, LANES)
-        moved = rolled(piece_rows, rest)
-        tiles[tile] = moved if tiles[tile] is None else jnp.where(lanes >= rest, moved, tiles[tile])
-        if rest + head_dim > LANES:
-            tiles[tile + 1] = moved
-    attended = jnp.concatenate(tiles, axis=1)
-    gated = (attended * jax.nn.sigmoid(gate_s[...].astype(jnp.float32))).astype(jnp.bfloat16)
-    cond = jnp.dot(gated, w_oc[0], preferred_element_type=jnp.float32) + jnp.dot(
-        gated, w_oc[1], preferred_element_type=jnp.float32
-    )
-    cond_rim[2] = cond.astype(jnp.bfloat16)
-    cond_sends = [
-        near_copy(cond_rim.at[2], cond_rim.at[1], 1, 4),
-        near_copy(cond_rim.at[2], cond_rim.at[0], 2, 5),
-        near_copy(cond_rim.at[2], cond_rim.at[3], -1, 6),
-    ]
-    for copy in cond_sends:
-        copy.start()
-    update = jnp.dot(gated, wo[...], preferred_element_type=jnp.float32)
-    update_ref[...] = update.reshape(samples, tokens, width).astype(jnp.bfloat16)
-    for copy in cond_sends:
-        copy.wait_recv()
-
-    conds = [
-        cond_rim[b].astype(jnp.float32).reshape(samples, tokens, atom_width) for b in range(4)
-    ]
+    gate_recv[my_slot] = gate_send[my_core, my_head]
+
+    ring_steps(3, 7)
+    atom_setup()
+    ring_steps(7, 10)
+    weight_product()
+    bias_pass()
+    ring_steps(10, 14)
+    bias_stage()
+    wait_some(gate_recv, peers - 1, a2a_recv_sem.at[6])
+    for s in range(per_core):
+        if s < 3:
+            ring_steps(14 + s, 15 + s)
+        complete(s)
+        attend(s)
+        if s == 2:
+            ring_steps(17, 18)
+            send_early()
+            ring_steps(18, 20)
+    send_late()
+
     chooser = selector[:, : 4 * tokens]
     atom_gain = again_ref[...].reshape(1, atom_width)
     shares = jnp.full((2 * atom_width, atom_width), 1.0 / atom_width, jnp.bfloat16)
@@ -607,8 +729,8 @@
             jnp.concatenate([high, low], axis=1), shares, preferred_element_type=jnp.float32
         )
 
-    for s in range(samples):
-        near_cond = jnp.concatenate([conds[b][s] for b in range(4)], axis=0).astype(jnp.bfloat16)
+    def atom_project(s, blocks):
+        near_cond = jnp.concatenate(blocks, axis=0).astype(jnp.bfloat16)
         carried = jnp.dot(chooser, near_cond, preferred_element_type=jnp.float32)
         state = atoms[s].astype(jnp.float32) + carried
         own_state = state[reach : reach + atom_dev]
@@ -661,44 +783,66 @@
                 joined[:, :atom_width] / joined[:, atom_width:] * jax.nn.sigmoid(gate)
             ).astype(jnp.bfloat16)
 
-    def atom_step(i, carry):
-        for half in range(2):
-            atom_attend(2 * i + half)
-        return carry
-
-    lax.fori_loop(0, samples // 2, atom_step, 0)
-
     local = token_ref[...] - (device - 1) * tokens
     gather = (local == lax.broadcasted_iota(jnp.int32, (2 * tokens, atom_dev), 0)).astype(
         jnp.bfloat16
     )
-    sums = []
-    for s in range(samples):
-        result = (
-            state_s[s] + jnp.dot(gated_s[s], w_ao[...], preferred_element_type=jnp.float32)
-        ).astype(jnp.bfloat16)
-        result_ref[s] = result
-        sums.append(jnp.dot(gather, result, preferred_element_type=jnp.float32))
+    sums = [None] * samples
+
+    def atom_pass(conds, members):
+        for core in range(2):
+            for i, s in enumerate(members):
+                atom_project(core * per_core + s, [conds[b, core, i] for b in range(4)])
+
+        def atom_step(i, carry):
+            for core in range(2):
+                atom_attend(core * per_core + i)
+            return carry
+
+        lax.fori_loop(members[0], members[-1] + 1, atom_step, 0)
+        for core in range(2):
+            for i in members:
+                s = core * per_core + i
+                result = (
+                    state_s[s] + jnp.dot(gated_s[s], w_ao[...], preferred_element_type=jnp.float32)
+                ).astype(jnp.bfloat16)
+                result_ref[s] = result
+                sums[s] = jnp.dot(gather, result, preferred_element_type=jnp.float32)
+
+    wait_results(early_recv, 2)
+    atom_pass(condition(early_rows, early, own_early), early)
+    wait_results(late_recv, 3)
+    atom_pass(condition(late_rows, late, own_late), late)
     pool_send[...] = jnp.concatenate([one[:tokens] for one in sums], axis=0).astype(jnp.bfloat16)
     pool_copy = near_copy(pool_send, pool_recv, -1, 7)
     pool_copy.start()
+    n_early, n_late = len(early) * tokens, len(late) * tokens
+    gated = jnp.concatenate(
+        [
+            rows[core * count : (core + 1) * count]
+            for core in range(2)
+            for rows, count in ((own_early[...], n_early), (own_late[...], n_late))
+        ],
+        axis=0,
+    ).astype(jnp.bfloat16)
+    update = jnp.dot(gated, wo[...], preferred_element_type=jnp.float32)
+    update_ref[...] = update.reshape(samples, tokens, width).astype(jnp.bfloat16)
     pool_copy.wait_recv()
     arrived = jnp.where(device < devices - 1, pool_recv[...].astype(jnp.float32), 0.0)
     own_sums = jnp.concatenate([one[tokens:] for one in sums], axis=0) + arrived
     sums_ref[...] = own_sums
-    for copy in near_sends + cond_sends + [pool_copy, bias_forward]:
+    for copy in near_sends + [pool_copy, bias_forward]:
         copy.wait_send()
     wait_some(qkv_recv, peers - 1, a2a_send_sem.at[0])
     wait_some(bias_send, heads - 1, a2a_send_sem.at[1])
-    wait_some(out_recv, peers - 1, a2a_send_sem.at[2])
-
-    def drain(s, carry):
-        for way in range(2):
-            for hop in range(1, half_ring + 1):
-                ring_send(way, hop, s).wait_send()
-        return carry
-
-    lax.fori_loop(0, per_core, drain, 0)
+    wait_some(gate_recv, peers - 1, a2a_send_sem.at[4])
+    wait_some(early_recv.at[0], peers - 1, a2a_send_sem.at[2])
+    wait_some(late_recv.at[0], peers - 1, a2a_send_sem.at[3])
+    for copy in early_copies[1] + late_copies[1]:
+        copy.wait_send()
+
+    for hop, s in steps[-in_flight:]:
+        settle(hop, s)
 
 
 def finish_kernel(sums_ref, gain_ref, weight_ref, update_in, result_in, update, result, pool):
@@ -764,9 +908,14 @@
             pltpu.VMEM((planes, per_core, 2 * head_dim, plane_tokens), bf16),
             pltpu.VMEM((planes, plane_tokens, plane_tokens), f32),
             pltpu.VMEM((per_core, plane_tokens, LANES), f32),
-            pltpu.VMEM((peers, 2 * tokens, LANES), bf16),
-            pltpu.VMEM((peers, 2 * tokens, LANES), bf16),
-            pltpu.VMEM((samples * tokens, width), bf16),
+            pltpu.VMEM((peers + 3, 6 * tokens, LANES), bf16),
+            pltpu.VMEM((2, peers, 6 * tokens, LANES), bf16),
+            pltpu.VMEM((peers + 3, 4 * tokens, LANES), bf16),
+            pltpu.VMEM((2, peers, 4 * tokens, LANES), bf16),
+            pltpu.VMEM((2, heads, 4 * tokens, LANES), bf16),
+            pltpu.VMEM((peers, 4 * tokens, LANES), bf16),
+            pltpu.VMEM((2 * 3 * tokens, width), f32),
+            pltpu.VMEM((2 * (per_core - 3) * tokens, width), f32),
             pltpu.VMEM((2,) + w_cond.shape, bf16),
             pltpu.VMEM((samples, ext, atom_width), bf16),
             pltpu.VMEM((2, 1, atom_dev), jnp.int32),
@@ -776,7 +925,6 @@
             pltpu.VMEM((atom_width, 2 * atom_width), bf16),
             pltpu.VMEM(atom_out.shape, bf16),
             pltpu.VMEM((ext, atom_dev), bf16),
-            pltpu.VMEM((4, samples * tokens, atom_width), bf16),
             pltpu.VMEM((samples, atom_dev, atom_width), f32),
             pltpu.VMEM((samples, ext, 2 * atom_width), bf16),
             pltpu.VMEM((samples, atom_dev, 2 * atom_width), bf16),
@@ -784,10 +932,11 @@
             pltpu.VMEM((samples * tokens, atom_width), bf16),
             pltpu.VMEM((samples * tokens, atom_width), bf16),
             pltpu.SemaphoreType.DMA((14,)),
-            pltpu.SemaphoreType.DMA((3,)),
-            pltpu.SemaphoreType.DMA((3,)),
+            pltpu.SemaphoreType.DMA((5,)),
+            pltpu.SemaphoreType.DMA((7,)),
             pltpu.SemaphoreType.DMA((2, planes // 2, per_core)),
             pltpu.SemaphoreType.DMA((2, planes // 2, per_core)),
+            pltpu.SemaphoreType.DMA((2, 3)),
             pltpu.SemaphoreType.DMA((9,)),
             pltpu.SemaphoreType.DMA((9,)),
         ],

time: 75.4 us -> 68.5 us (0.908)
  Pallas kernels: 74.7 us -> 67.7 us
    pallas_call x1, Pallas kernels: 72.5 us -> 65.6 us  [diffusion_pass(): pl.pallas_call(functools.partial(pass_kernel, heads, rows_plane, planes,...]
where the time goes in v4:
time: 68.5 us; the launch traced here: 68.4 us
  Pallas kernels  67.7 us (99%)
    pallas_call x1, Pallas kernels, diffusion_pass(): pl.pallas_call(functools.partial(pass_kernel, heads, rows_plane, planes,...  65.6 us
    pallas_call x1, Pallas kernels, diffusion_pass(): pl.pallas_call(finish_kernel, out_shape=(jax.ShapeDtypeStruct(update.shap...  2.18 us

profile of v4, /device:TPU:6, one launch (start us, length us, event | category | flops | bytes accessed | tf_op | source)
XLA Modules:
  0.0 68.4 jit_solution(4039614370976177256)
XLA Ops:
  0.6 65.6 %shard_map.211 = (bf16[10,8,768]{2,1,0:T(8,128)(2,1)}, bf16[10,128,128]{2,1,0:T(8,128)(2,1)}, f32[80,128]{1,0:T(8,128)}) custom-call(bf16[10,8,768]{2,1,0:T(8,128)(2,1)} %x_ref.1, f32[768]{0:T(1024)} %gain_ref.2, bf16[64,8,512]{2,1,0:T(8,128)(2,1)} %bias_hbm.1, bf16[768,768]{1,0:T(8,128)(2,1)} %wq_hbm.1, bf16[768,768]{1,0:T(8,128)(2,1)} %wk_hbm.1, ...), custom_call_target="tpu_custom_call" | custom-call | tf_op jit(solution)/shard_map/pallas_call | solution.py:880
  66.2 2.2 %shard_map.212 = (bf16[10,8,768]{2,1,0:T(8,128)(2,1)}, bf16[10,128,128]{2,1,0:T(8,128)(2,1)}, bf16[10,8,768]{2,1,0:T(8,128)(2,1)}) custom-call(f32[80,128]{1,0:T(8,128)} %get-tuple-element.6.sums_ref, f32[128]{0:T(128)} %gain_ref.3, bf16[128,768]{1,0:T(8,128)(2,1)} %weight_ref.1, bf16[10,8,768]{2,1,0:T(8,128)(2,1)} %get-tuple-element.7.update_in, ...), custom_call_target="tpu_custom_call" | custom-call | tf_op jit(solution)/shard_map/pallas_call | solution.py:966

commit v5 on v4

--- a/solution.py
+++ b/solution.py
@@ -82,6 +82,8 @@
     qkv_recv,
     kv_ring,
     scores,
+    peaks,
+    queries_kept,
     out_f,
     early_send,
     early_recv,
@@ -281,6 +283,19 @@
         ).start()
     qkv_recv[my_slot] = qkv_send[my_core, my_head]
 
+    near_sends = [
+        near_copy(
+            atom_hbm.at[:, pl.ds(atom_dev - reach, reach)], atoms.at[:, pl.ds(0, reach)], 1, 0
+        ),
+        near_copy(
+            atom_hbm.at[:, pl.ds(0, reach)], atoms.at[:, pl.ds(reach + atom_dev, reach)], -1, 1
+        ),
+        near_copy(token_ref, token_rim.at[0], 1, 2),
+        near_copy(token_ref, token_rim.at[1], -1, 3),
+    ]
+    for copy in near_sends:
+        copy.start()
+
     loads[4].wait()
     gate = jnp.dot(normed, wg[...], preferred_element_type=jnp.float32)
     for head in range(heads):
@@ -339,20 +354,6 @@
     bias_send[...] = bias_t[...].astype(jnp.bfloat16).reshape(heads, piece, LANES)
 
 
-    near_sends = [
-        near_copy(
-            atom_hbm.at[:, pl.ds(atom_dev - reach, reach)], atoms.at[:, pl.ds(0, reach)], 1, 0
-        ),
-        near_copy(
-            atom_hbm.at[:, pl.ds(0, reach)], atoms.at[:, pl.ds(reach + atom_dev, reach)], -1, 1
-        ),
-        near_copy(token_ref, token_rim.at[0], 1, 2),
-        near_copy(token_ref, token_rim.at[1], -1, 3),
-    ]
-    for copy in near_sends:
-        copy.start()
-
-
     def wait_some(buffer, count, sem):
         view = buffer.at[pl.ds(0, count)]
         pltpu.make_async_copy(view, view, sem).wait()
@@ -484,7 +485,7 @@
         w_oc[0] = high
         w_oc[1] = (product - high.astype(jnp.float32)).astype(jnp.bfloat16)
 
-    def attend(s):
+    def score(s):
         below = qkv_recv[:, part - tokens :, :].astype(jnp.float32)[:, tokens:, :]
         q_lanes = lane_index((plane_tokens, LANES))
         q_one = jnp.where(
@@ -492,17 +493,26 @@
             rolled(by_row(sample_rows(s)), spare),
             rolled(by_row(below), spare - s * rest_dim),
         ).astype(jnp.bfloat16)[:, :head_dim]
-        peak = None
-        for zz in range(planes):
-            raw = jnp.dot(q_one, kv_ring[zz, s, :head_dim, :], preferred_element_type=jnp.float32)
-            score = raw * factor + bias_all[zz]
-            scores[zz] = score
-            peak = score if peak is None else jnp.maximum(peak, score)
-        peak = jnp.max(peak, axis=-1, keepdims=True)
+        for ahead in range(planes):
+            if ahead != half_ring:
+                score_block(q_one, s, ahead)
+        queries_kept[s % 2] = q_one
+
+    def score_block(q_one, s, ahead):
+        zz = lax.rem(z + ahead, planes)
+        raw = jnp.dot(q_one, kv_ring[zz, s, :head_dim, :], preferred_element_type=jnp.float32)
+        score = raw * factor + bias_all[zz]
+        scores[s % 2, ahead] = score
+        peaks[s % 2] = score if ahead == 0 else jnp.maximum(peaks[s % 2], score)
+
+    def attend(s):
+        score_block(queries_kept[s % 2], s, half_ring)
+        peak = jnp.max(peaks[s % 2], axis=-1, keepdims=True)
         total = None
         ones = jnp.ones((LANES - head_dim, plane_tokens), jnp.bfloat16)
-        for zz in range(planes):
-            weights = jnp.exp2(scores[zz] - peak).astype(jnp.bfloat16)
+        for ahead in range(planes):
+            zz = lax.rem(z + ahead, planes)
+            weights = jnp.exp2(scores[s % 2, ahead] - peak).astype(jnp.bfloat16)
             v_one = jnp.concatenate([kv_ring[zz, s, head_dim:, :], ones], axis=0)
             mixed = lax.dot_general(
                 weights, v_one, (((1,), (1,)), ((), ())), preferred_element_type=jnp.float32
@@ -672,6 +682,7 @@
         )
         return cond.reshape(4, 2, len(members), tokens, atom_width)
 
+    weight_product()
     wait_some(qkv_recv, peers - 1, a2a_recv_sem.at[0])
     early, late = range(3), range(3, per_core)
     ring_steps(0, 3)
@@ -702,7 +713,6 @@
     ring_steps(3, 7)
     atom_setup()
     ring_steps(7, 10)
-    weight_product()
     bias_pass()
     ring_steps(10, 14)
     bias_stage()
@@ -710,6 +720,10 @@
     for s in range(per_core):
         if s < 3:
             ring_steps(14 + s, 15 + s)
+        if s != 4:
+            score(s)
+        if s == 3:
+            score(4)
         complete(s)
         attend(s)
         if s == 2:
@@ -799,7 +813,11 @@
                 atom_attend(core * per_core + i)
             return carry
 
-        lax.fori_loop(members[0], members[-1] + 1, atom_step, 0)
+        if len(members) == 3:
+            lax.fori_loop(members[0], members[-1] + 1, atom_step, 0)
+        else:
+            for i in members:
+                atom_step(i, 0)
         for core in range(2):
             for i in members:
                 s = core * per_core + i
@@ -906,7 +924,9 @@
             pltpu.VMEM((2, heads, padded, LANES), bf16),
             pltpu.VMEM((peers, padded, LANES), bf16),
             pltpu.VMEM((planes, per_core, 2 * head_dim, plane_tokens), bf16),
-            pltpu.VMEM((planes, plane_tokens, plane_tokens), f32),
+            pltpu.VMEM((2, planes, plane_tokens, plane_tokens), f32),
+            pltpu.VMEM((2, plane_tokens, plane_tokens), f32),
+            pltpu.VMEM((2, plane_tokens, head_dim), bf16),
             pltpu.VMEM((per_core, plane_tokens, LANES), f32),
             pltpu.VMEM((peers + 3, 6 * tokens, LANES), bf16),
             pltpu.VMEM((2, peers, 6 * tokens, LANES), bf16),

time: 68.5 us -> 67.3 us (0.982)
  Pallas kernels: 67.7 us -> 66.5 us
    pallas_call x1, Pallas kernels: 65.6 us -> 64.3 us  [diffusion_pass(): pl.pallas_call(functools.partial(pass_kernel, heads, rows_plane, planes,...]
where the time goes in v5:
time: 67.3 us; the launch traced here: 67.1 us
  Pallas kernels  66.5 us (99%)
    pallas_call x1, Pallas kernels, diffusion_pass(): pl.pallas_call(functools.partial(pass_kernel, heads, rows_plane, planes,...  64.3 us
    pallas_call x1, Pallas kernels, diffusion_pass(): pl.pallas_call(finish_kernel, out_shape=(jax.ShapeDtypeStruct(update.shap...  2.18 us

profile of v5, /device:TPU:6, one launch (start us, length us, event | category | flops | bytes accessed | tf_op | source)
XLA Modules:
  0.0 67.1 jit_solution(6659724117308760123)
XLA Ops:
  0.6 64.3 %shard_map.211 = (bf16[10,8,768]{2,1,0:T(8,128)(2,1)}, bf16[10,128,128]{2,1,0:T(8,128)(2,1)}, f32[80,128]{1,0:T(8,128)}) custom-call(bf16[10,8,768]{2,1,0:T(8,128)(2,1)} %x_ref.1, f32[768]{0:T(1024)} %gain_ref.2, bf16[64,8,512]{2,1,0:T(8,128)(2,1)} %bias_hbm.1, bf16[768,768]{1,0:T(8,128)(2,1)} %wq_hbm.1, bf16[768,768]{1,0:T(8,128)(2,1)} %wk_hbm.1, ...), custom_call_target="tpu_custom_call" | custom-call | tf_op jit(solution)/shard_map/pallas_call | solution.py:898
  64.9 2.2 %shard_map.212 = (bf16[10,8,768]{2,1,0:T(8,128)(2,1)}, bf16[10,128,128]{2,1,0:T(8,128)(2,1)}, bf16[10,8,768]{2,1,0:T(8,128)(2,1)}) custom-call(f32[80,128]{1,0:T(8,128)} %get-tuple-element.6.sums_ref, f32[128]{0:T(128)} %gain_ref.3, bf16[128,768]{1,0:T(8,128)(2,1)} %weight_ref.1, bf16[10,8,768]{2,1,0:T(8,128)(2,1)} %get-tuple-element.7.update_in, ...), custom_call_target="tpu_custom_call" | custom-call | tf_op jit(solution)/shard_map/pallas_call | solution.py:986

commit v6 on v5

--- a/solution.py
+++ b/solution.py
@@ -317,7 +317,7 @@
     columns = bias_in.shape[2]
     flat_bias = bias_in[...].astype(jnp.float32).reshape(queries * tokens, columns)
     for tile in range(columns // LANES):
-        bias_f[tile] = flat_bias[:, tile * LANES : (tile + 1) * LANES]
+        bias_f[tile, : queries * tokens, :] = flat_bias[:, tile * LANES : (tile + 1) * LANES]
     rho = lax.broadcasted_iota(jnp.int32, (columns, columns), 0)
     lam = lane_index((columns, columns))
     ylo, rest = rho // (columns // 2), rho % (columns // 2)
@@ -351,7 +351,7 @@
             low, pltpu.roll(top, queries, 1), bottom
         )
     piece = planes * 2 * tokens
-    bias_send[...] = bias_t[...].astype(jnp.bfloat16).reshape(heads, piece, LANES)
+    bias_send[...] = bias_t[: heads * piece, :].astype(jnp.bfloat16).reshape(heads, piece, LANES)
 
 
     def wait_some(buffer, count, sem):
@@ -915,8 +915,8 @@
             pltpu.VMEM(w_gate.shape, bf16),
             pltpu.VMEM(w_out.shape, bf16),
             pltpu.VMEM(w_cond.shape, bf16),
-            pltpu.VMEM((columns // LANES, queries * tokens, LANES), f32),
-            pltpu.VMEM((heads * piece, LANES), f32),
+            pltpu.VMEM((columns // LANES, (queries + 1) * tokens, LANES), f32),
+            pltpu.VMEM((heads * piece + tokens, LANES), f32),
             pltpu.VMEM((heads, piece, LANES), bf16),
             pltpu.VMEM((2, heads, piece, LANES), bf16),
             pltpu.VMEM((planes, n_col, 2, 2 * tokens, plane_tokens), bf16),

time: 67.3 us -> 67.3 us (level)
  no operation moved by 1% of the time
where the time goes in v6:
time: 67.3 us; the launch traced here: 67.2 us
  Pallas kernels  66.5 us (99%)
    pallas_call x1, Pallas kernels, diffusion_pass(): pl.pallas_call(functools.partial(pass_kernel, heads, rows_plane, planes,...  64.3 us
    pallas_call x1, Pallas kernels, diffusion_pass(): pl.pallas_call(finish_kernel, out_shape=(jax.ShapeDtypeStruct(update.shap...  2.18 us

profile of v6, /device:TPU:6, one launch (start us, length us, event | category | flops | bytes accessed | tf_op | source)
XLA Modules:
  0.0 67.2 jit_solution(16489998867533956832)
XLA Ops:
  0.6 64.3 %shard_map.211 = (bf16[10,8,768]{2,1,0:T(8,128)(2,1)}, bf16[10,128,128]{2,1,0:T(8,128)(2,1)}, f32[80,128]{1,0:T(8,128)}) custom-call(bf16[10,8,768]{2,1,0:T(8,128)(2,1)} %x_ref.1, f32[768]{0:T(1024)} %gain_ref.2, bf16[64,8,512]{2,1,0:T(8,128)(2,1)} %bias_hbm.1, bf16[768,768]{1,0:T(8,128)(2,1)} %wq_hbm.1, bf16[768,768]{1,0:T(8,128)(2,1)} %wk_hbm.1, ...), custom_call_target="tpu_custom_call" | custom-call | tf_op jit(solution)/shard_map/pallas_call | solution.py:898
  65.0 2.2 %shard_map.212 = (bf16[10,8,768]{2,1,0:T(8,128)(2,1)}, bf16[10,128,128]{2,1,0:T(8,128)(2,1)}, bf16[10,8,768]{2,1,0:T(8,128)(2,1)}) custom-call(f32[80,128]{1,0:T(8,128)} %get-tuple-element.6.sums_ref, f32[128]{0:T(128)} %gain_ref.3, bf16[128,768]{1,0:T(8,128)(2,1)} %weight_ref.1, bf16[10,8,768]{2,1,0:T(8,128)(2,1)} %get-tuple-element.7.update_in, ...), custom_call_target="tpu_custom_call" | custom-call | tf_op jit(solution)/shard_map/pallas_call | solution.py:986
